TPU v7x, 32 devices: a whole 2x2x4 slice. The times are simulated.
32 devices in a mesh: ctx: 4 (over x, core), ch: 8 (over z, y).
Axes of the slice: x: 2, y: 2, z: 4, core: 2. Of those that a mesh axis runs over, the one named last changes fastest.
Arguments:
- query_gate: bfloat16 [1024, 8192], P(('ctx', 'ch')), may hold values from -6 to 6
- key_gate: bfloat16 [1024, 8192], P(('ctx', 'ch')), may hold values from -6 to 6
- value_proj: bfloat16 [1024, 8192], P(('ctx', 'ch')), may hold values from -6 to 6
- grad_out: bfloat16 [1024, 8192], P(('ctx', 'ch')), may hold values from -0.375 to 0.375
- long_filters: float32 [512, 1024], P('ch', 'ctx'), may hold values from -0.1875 to 0.1875
Outputs:
- grad_query: bfloat16 [1024, 8192], P(('ctx', 'ch'))
- grad_key: bfloat16 [1024, 8192], P(('ctx', 'ch'))
- grad_value: bfloat16 [1024, 8192], P(('ctx', 'ch'))
- grad_filters: float32 [512, 1024], P('ch', 'ctx')
All inputs are finite; a program needn't handle non-finite values.
Results may differ from a plain program's by a relative error of at most 0.0058.
Values may be sent and summed in bfloat16 or wider, within the bound.
A program may use at most 64 MiB of HBM per device.

v0:
```python
import math

import jax
import jax.numpy as jnp
from jax import lax
from jax.sharding import PartitionSpec as P

GROUP_CH = 16


HIGHEST_MODE = lax.Precision.HIGHEST
SPLIT_MODE = lax.Precision.HIGH


def passed_along(value, axis, steps):
    count = lax.axis_size(axis)
    leading, last = (max(0, -steps), min(count, count - steps))
    return lax.ppermute(value, axis, [(source, source + steps) for source in range(leading, last)])


def make_tables(block_len):
    period = 2 * block_len
    steps = lax.iota(jnp.int32, block_len)
    phase = steps[:, None] * steps[None, :] % period
    angle = phase.astype(jnp.float32) * (math.pi / block_len)
    cosine = jnp.cos(angle)
    sine = jnp.sin(angle)
    parity = 1.0 - 2.0 * (steps % 2).astype(jnp.float32)
    weights = jnp.where(steps == 0, 1.0, 2.0).astype(jnp.float32) / period
    return (
        cosine,
        -sine,
        parity,
        cosine * weights[None, :],
        -sine * weights[None, :],
        parity / period,
    )


def columns_forward(tables, values):
    return (
        jnp.dot(tables[0], values, precision=SPLIT_MODE),
        jnp.dot(tables[1], values, precision=SPLIT_MODE),
        jnp.dot(tables[2], values, precision=SPLIT_MODE),
    )


def columns_inverse(tables, real_part, imag_part, nyquist):
    return (
        jnp.dot(tables[3], real_part, precision=SPLIT_MODE)
        + jnp.dot(tables[4], imag_part, precision=SPLIT_MODE)
        + tables[5][:, None] * nyquist[None, :]
    )


def rows_forward(tables, values):
    return (
        jnp.dot(values, tables[0], precision=HIGHEST_MODE),
        jnp.dot(values, tables[1], precision=HIGHEST_MODE),
        jnp.dot(values, tables[2], precision=HIGHEST_MODE),
    )


def rows_inverse(tables, real_part, imag_part, nyquist):
    return (
        jnp.dot(real_part, tables[3].T, precision=SPLIT_MODE)
        + jnp.dot(imag_part, tables[4].T, precision=SPLIT_MODE)
        + nyquist[:, None] * tables[5][None, :]
    )


def spread_groups(rows):
    groups, block_len = rows.shape
    return jnp.broadcast_to(rows.T[:, :, None], (block_len, groups, GROUP_CH)).reshape(
        block_len, groups * GROUP_CH
    )


def spread_vector(vector):
    return jnp.broadcast_to(vector[:, None], (vector.shape[0], GROUP_CH)).reshape(-1)


def group_rows(matrix):
    block_len, chans = matrix.shape
    return matrix.reshape(block_len, chans // GROUP_CH, GROUP_CH).sum(axis=2).T


def group_vector(vector):
    return vector.reshape(-1, GROUP_CH).sum(axis=1)


def by_blocks(tables, signal, upstream, long_filters):
    block_len, chans = signal.shape
    groups = long_filters.shape[0]
    nblocks = lax.axis_size("ctx")
    own_block = lax.axis_index("ctx")
    parity = tables[2]
    prev_taps = passed_along(long_filters, "ctx", 1)
    both_re, both_im, both_ny = rows_forward(
        tables, jnp.concatenate([prev_taps, long_filters], axis=0)
    )
    own_re = both_re[:groups] + both_re[groups:] * parity
    own_im = both_im[:groups] + both_im[groups:] * parity
    own_ny = both_ny[:groups] + both_ny[groups:]
    lag_re, lag_im, lag_ny = (
        lax.all_gather(own_re[None], "ctx", axis=0, tiled=True),
        lax.all_gather(own_im[None], "ctx", axis=0, tiled=True),
        lax.all_gather(own_ny[None], "ctx", axis=0, tiled=True),
    )
    mine_re, mine_im, mine_ny = columns_forward(tables, upstream.astype(jnp.float32))
    mine_re = mine_re * parity[:, None]
    mine_im = mine_im * parity[:, None]

    def pick(lag_index):
        return (
            spread_groups(lax.dynamic_index_in_dim(lag_re, lag_index, 0, keepdims=False)),
            spread_groups(lax.dynamic_index_in_dim(lag_im, lag_index, 0, keepdims=False)),
            spread_vector(lax.dynamic_index_in_dim(lag_ny, lag_index, 0, keepdims=False)),
        )

    def add_earlier(totals, block_vals, lag_index):
        conv_re, conv_im, conv_ny, back_re, back_im, back_ny, corr_re, corr_im, corr_ny = totals
        sig_re, sig_im, sig_ny = columns_forward(tables, block_vals)
        tap_re, tap_im, tap_ny = pick(lag_index)
        conv_re = conv_re + tap_re * sig_re - tap_im * sig_im
        conv_im = conv_im + tap_re * sig_im + tap_im * sig_re
        conv_ny = conv_ny + tap_ny * sig_ny
        corr_re = corr_re.at[lag_index].add(group_rows(mine_re * sig_re + mine_im * sig_im))
        corr_im = corr_im.at[lag_index].add(group_rows(mine_im * sig_re - mine_re * sig_im))
        corr_ny = corr_ny.at[lag_index].add(group_vector(mine_ny * sig_ny))
        return (conv_re, conv_im, conv_ny, back_re, back_im, back_ny, corr_re, corr_im, corr_ny)

    def add_later(totals, block_vals, lag_index):
        conv_re, conv_im, conv_ny, back_re, back_im, back_ny, corr_re, corr_im, corr_ny = totals
        up_re, up_im, up_ny = columns_forward(tables, block_vals)
        up_re = up_re * parity[:, None]
        up_im = up_im * parity[:, None]
        tap_re, tap_im, tap_ny = pick(lag_index)
        back_re = back_re + tap_re * up_re + tap_im * up_im
        back_im = back_im + tap_re * up_im - tap_im * up_re
        back_ny = back_ny + tap_ny * up_ny
        return (conv_re, conv_im, conv_ny, back_re, back_im, back_ny, corr_re, corr_im, corr_ny)

    plane = jnp.zeros((block_len, chans), jnp.float32)
    edge = jnp.zeros((chans,), jnp.float32)
    stack = jnp.zeros((nblocks, groups, block_len), jnp.float32)
    stack_edge = jnp.zeros((nblocks, groups), jnp.float32)
    initial = (plane, plane, edge, plane, plane, edge, stack, stack, stack_edge)
    sig_piece = lax.all_gather(signal, "ctx", axis=0, tiled=True)
    up_piece = lax.all_gather(upstream, "ctx", axis=0, tiled=True)
    piece_blocks = sig_piece.shape[0] // block_len

    def one_block(offset, running):
        sig_vals = lax.dynamic_slice_in_dim(sig_piece, offset * block_len, block_len, 0).astype(
            jnp.float32
        )
        up_vals = lax.dynamic_slice_in_dim(up_piece, offset * block_len, block_len, 0).astype(
            jnp.float32
        )
        running = lax.cond(
            offset <= own_block,
            lambda current: add_earlier(current, sig_vals, own_block - offset),
            lambda current: current,
            running,
        )
        running = lax.cond(
            offset >= own_block,
            lambda current: add_later(current, up_vals, offset - own_block),
            lambda current: current,
            running,
        )
        return running

    totals = lax.fori_loop(0, piece_blocks, one_block, initial)
    conv_re, conv_im, conv_ny, back_re, back_im, back_ny, corr_re, corr_im, corr_ny = totals
    convolved = columns_inverse(
        tables, conv_re * parity[:, None], conv_im * parity[:, None], conv_ny
    )
    correlated = columns_inverse(tables, back_re, back_im, back_ny)
    total_re, total_im, total_ny = lax.psum((corr_re, corr_im, corr_ny), "ctx")
    next_block = jnp.minimum(own_block + 1, nblocks - 1)
    valid = (own_block + 1 < nblocks).astype(jnp.float32)
    cur_re = lax.dynamic_index_in_dim(total_re, own_block, 0, keepdims=False)
    cur_im = lax.dynamic_index_in_dim(total_im, own_block, 0, keepdims=False)
    cur_ny = lax.dynamic_index_in_dim(total_ny, own_block, 0, keepdims=False)
    nxt_re = lax.dynamic_index_in_dim(total_re, next_block, 0, keepdims=False)
    nxt_im = lax.dynamic_index_in_dim(total_im, next_block, 0, keepdims=False)
    nxt_ny = lax.dynamic_index_in_dim(total_ny, next_block, 0, keepdims=False)
    upper = rows_inverse(tables, cur_re * parity, cur_im * parity, cur_ny)
    lower = rows_inverse(tables, nxt_re, nxt_im, nxt_ny)
    grad_filters = upper + lower * valid
    return (convolved, correlated, grad_filters)


def on_device(query_gate, key_gate, value_proj, grad_out, long_filters):
    query_cols, key_cols, value_cols, grad_cols = (
        lax.all_to_all(query_gate, "ch", split_axis=1, concat_axis=0, tiled=True),
        lax.all_to_all(key_gate, "ch", split_axis=1, concat_axis=0, tiled=True),
        lax.all_to_all(value_proj, "ch", split_axis=1, concat_axis=0, tiled=True),
        lax.all_to_all(grad_out, "ch", split_axis=1, concat_axis=0, tiled=True),
    )
    query_vals = query_cols.astype(jnp.float32)
    key_vals = key_cols.astype(jnp.float32)
    value_vals = value_cols.astype(jnp.float32)
    grad_vals = grad_cols.astype(jnp.float32)
    signal = (key_vals * value_vals).astype(jnp.bfloat16)
    upstream = (grad_vals * query_vals).astype(jnp.bfloat16)
    tables = make_tables(signal.shape[0])
    convolved, correlated, grad_filters = by_blocks(tables, signal, upstream, long_filters)
    conv_half = convolved.astype(jnp.bfloat16)
    corr_half = correlated.astype(jnp.bfloat16)
    conv_wide = lax.optimization_barrier(conv_half).astype(jnp.float32)
    corr_wide = lax.optimization_barrier(corr_half).astype(jnp.float32)
    grad_query = (grad_vals * conv_wide).astype(jnp.bfloat16)
    grad_key = (corr_wide * value_vals).astype(jnp.bfloat16)
    grad_value = (corr_wide * key_vals).astype(jnp.bfloat16)
    query_rows, key_rows, value_rows = (
        lax.all_to_all(grad_query, "ch", split_axis=0, concat_axis=1, tiled=True),
        lax.all_to_all(grad_key, "ch", split_axis=0, concat_axis=1, tiled=True),
        lax.all_to_all(grad_value, "ch", split_axis=0, concat_axis=1, tiled=True),
    )
    return (query_rows, key_rows, value_rows, grad_filters)


def solution(mesh):
    in_specs = (
        P(("ctx", "ch"), None),
        P(("ctx", "ch"), None),
        P(("ctx", "ch"), None),
        P(("ctx", "ch"), None),
        P("ch", "ctx"),
    )
    out_specs = (
        P(("ctx", "ch"), None),
        P(("ctx", "ch"), None),
        P(("ctx", "ch"), None),
        P("ch", "ctx"),
    )
    return jax.shard_map(
        on_device, mesh=mesh, in_specs=in_specs, out_specs=out_specs, check_vma=False
    )
```

profile of v0, /device:TPU:0, one launch (start us, length us, event | category | flops | bytes accessed | tf_op | source)
XLA Modules:
  0.0 337.9 jit_solution(2176587224923924270)
XLA Ops:
  7.2 1.9 copy.49
  9.1 7.3 %all-to-all-start = ((bf16[32,8,1024]{2,0,1:T(8,128)(2,1)}), bf16[32,8,1024]{2,0,1:T(8,128)(2,1)S(1)}, u32[]{:S(2)}, u32[]{:S(2)}) async-start(bf16[32,8,1024]{2,0,1:T(8,128)(2,1)} %bitcast.141), calls=%async_computation | async-start | bytes 1048576 | tf_op jit(solution)/shard_map/all_to_all | solution.py:200
  16.5 14.4 %all-to-all-done = bf16[32,8,1024]{2,0,1:T(8,128)(2,1)S(1)} async-done(((bf16[32,8,1024]{2,0,1:T(8,128)(2,1)}), bf16[32,8,1024]{2,0,1:T(8,128)(2,1)S(1)}, u32[]{:S(2)}, u32[]{:S(2)}) %all-to-all-start) | async-done | bytes 524320 | tf_op jit(solution)/shard_map/all_to_all | solution.py:200
  30.9 18.1 %all_to_all.109 = bf16[32,8,1024]{2,0,1:T(8,128)(2,1)S(1)} all-to-all(bf16[32,8,1024]{2,0,1:T(8,128)(2,1)S(1)} %bitcast.151), channel_id=1, replica_groups=mesh['ctx'=4,'ch'=8] {'ch'}, dimensions={1} | all-to-all | bytes 1048576 | tf_op jit(solution)/shard_map/all_to_all | solution.py:197
  50.8 3.6 %all-to-all-start.1 = ((bf16[32,8,1024]{2,0,1:T(8,128)(2,1)}), bf16[32,8,1024]{2,0,1:T(8,128)(2,1)S(1)}, u32[]{:S(2)}, u32[]{:S(2)}) async-start(bf16[32,8,1024]{2,0,1:T(8,128)(2,1)} %bitcast.140), calls=%async_computation.1 | async-start | bytes 1048576 | tf_op jit(solution)/shard_map/all_to_all | solution.py:198
  54.6 14.1 %all-to-all-done.1 = bf16[32,8,1024]{2,0,1:T(8,128)(2,1)S(1)} async-done(((bf16[32,8,1024]{2,0,1:T(8,128)(2,1)}), bf16[32,8,1024]{2,0,1:T(8,128)(2,1)S(1)}, u32[]{:S(2)}, u32[]{:S(2)}) %all-to-all-start.1) | async-done | bytes 524320 | tf_op jit(solution)/shard_map/all_to_all | solution.py:198
  68.7 17.9 %all_to_all.110 = bf16[32,8,1024]{2,0,1:T(8,128)(2,1)S(1)} all-to-all(bf16[32,8,1024]{2,0,1:T(8,128)(2,1)S(1)} %bitcast.152), channel_id=1, replica_groups=mesh['ctx'=4,'ch'=8] {'ch'}, dimensions={1} | all-to-all | bytes 1048576 | tf_op jit(solution)/shard_map/all_to_all | solution.py:199
  91.5 8.3 %all-reduce = f32[256]{0:T(256)S(1)} all-reduce(f32[256]{0:T(256)S(1)} %add_dynamic-update-slice_fusion), channel_id=4, replica_groups=mesh['ctx'=4,'ch'=8] {'ctx'}, use_global_device_ids=true, to_apply=%add | all-reduce | flops 256 | bytes 2048
  102.5 8.5 %all-gather = f32[256,256]{1,0:T(8,128)} all-gather(f32[64,256]{1,0:T(8,128)S(1)} %get-tuple-element.758), channel_id=2, replica_groups=mesh['ctx'=4,'ch'=8] {'ctx'}, dimensions={0}, use_global_device_ids=true | all-gather | bytes 327680 | tf_op jit(solution)/shard_map/all_gather | solution.py:106
  111.0 6.3 %all-gather.1 = f32[256,256]{1,0:T(8,128)} all-gather(f32[64,256]{1,0:T(8,128)S(1)} %get-tuple-element.757), channel_id=3, replica_groups=mesh['ctx'=4,'ch'=8] {'ctx'}, dimensions={0}, use_global_device_ids=true | all-gather | bytes 327680 | tf_op jit(solution)/shard_map/all_gather | solution.py:107
  117.5 2.4 convolution_multiply_fusion.2
  119.9 2.4 convolution_multiply_fusion.3
  128.3 76.8 %while.34 = (s32[]{:T(128)}, f32[256,1024]{1,0:T(8,128)}, f32[256,1024]{1,0:T(8,128)}, f32[1024]{0:T(1024)S(1)}, f32[256,1024]{1,0:T(8,128)}, /*index=5*/f32[256...) while((s32[]{:T(128)}, f32[256,1024]{1,0:T(8,128)}, ...), condition=%wide.region_10.11_spmd.clone.clone, body=%wide.region_0.10_spmd.clone.clone.sunk | while | flops 1622122752 | bytes 82671808 | solution.py:174
  128.3 1.4 dynamic-slice_convert_fusion.3
  129.7 1.7 sine_negate_fusion.9
  131.5 26.4 %conditional.8 = ((f32[256,1024]{1,0:T(8,128)}, f32[256,1024]{1,0:T(8,128)}, f32[1024]{0:T(1024)S(1)}, f32[4,64,256]{2,1,0:T(8,128)}, f32[4,64,256]{2,1,0:T(8,128)}, /*index=5*/f32[4,64]{1,0:T(4,128)S(1)})) conditional(s32[]{:T(128)} %convert_element_type.320, (f32[256,1024]{1,0:T(8,128)}, f32[256,1024]{1,0:T(8,128)}, f32[1024]{0:T(1024)S(1)}, ...), branch_computations={%region_1.1_spmd, %region_2.7_spmd} | conditional | flops 811110464 | bytes 42394240 | solution.py:160
  133.4 1.6 copy.18
  136.9 2.6 copy.19
  139.4 1.7 fusion.138
  141.2 5.1 %multiply_subtract_fusion = (f32[256,1024]{1,0:T(8,128)}, f32[256,1024]{1,0:T(8,128)}, f32[256,1024]{1,0:T(8,128)}, f32[256,1024]{1,0:T(8,128)}) fusion(f32[256,1024]{1,0:T(8,128)} %get-tuple-element.482, f32[256,1024]{1,0:T(8,128)S(1)} %copy-done.8, f32[256,1024]{1,0:T(8,128)S(1)} %fusion.138, f32[256,1024]{1,0:T(8,128)S(1)} %copy-done.1, ...), kind=kOutput, calls=%fused_computation.5 | convolution fusion | flops 406323200 | bytes 12845056 | tf_op jit(solution)/shard_map/while/body/eval_jaxpr/cond/branch_1_fun/dot_general | solution.py:43
  146.3 2.6 copy.23
  153.8 2.1 fusion.6
  157.9 9.4 %conditional.9 = ((f32[256,1024]{1,0:T(8,128)}, f32[256,1024]{1,0:T(8,128)}, f32[1024]{0:T(1024)S(1)})) conditional(s32[]{:T(128)} %convert_element_type.321, (f32[256,1024]{1,0:T(8,128)}, f32[256,1024]{1,0:T(8,128)}, f32[1024]{0:T(1024)S(1)}) %tuple.96, (s32[]{:T(128)}, s32[]{:T(128)}, f32[4,64,256]{2,1,0:T(8,128)}, f32[256,256]{1,0:T(8,128)}, ...), branch_computations={%region_8.8_spmd, %region_9.9_spmd} | conditional | flops 809502720 | bytes 36605924 | solution.py:166
  160.3 1.6 copy.25
  167.4 1.4 dynamic-slice_convert_fusion.3
  168.8 1.7 sine_negate_fusion.9
  170.6 9.4 %conditional.9 = ((f32[256,1024]{1,0:T(8,128)}, f32[256,1024]{1,0:T(8,128)}, f32[1024]{0:T(1024)S(1)})) conditional(s32[]{:T(128)} %convert_element_type.321, (f32[256,1024]{1,0:T(8,128)}, f32[256,1024]{1,0:T(8,128)}, f32[1024]{0:T(1024)S(1)}) %tuple.96, (s32[]{:T(128)}, s32[]{:T(128)}, f32[4,64,256]{2,1,0:T(8,128)}, f32[256,256]{1,0:T(8,128)}, ...), branch_computations={%region_8.8_spmd, %region_9.9_spmd} | conditional | flops 809502720 | bytes 36605924 | solution.py:166
  172.9 1.6 copy.25
  180.0 1.4 dynamic-slice_convert_fusion.3
  181.4 1.7 sine_negate_fusion.9
  183.2 9.4 %conditional.9 = ((f32[256,1024]{1,0:T(8,128)}, f32[256,1024]{1,0:T(8,128)}, f32[1024]{0:T(1024)S(1)})) conditional(s32[]{:T(128)} %convert_element_type.321, (f32[256,1024]{1,0:T(8,128)}, f32[256,1024]{1,0:T(8,128)}, f32[1024]{0:T(1024)S(1)}) %tuple.96, (s32[]{:T(128)}, s32[]{:T(128)}, f32[4,64,256]{2,1,0:T(8,128)}, f32[256,256]{1,0:T(8,128)}, ...), branch_computations={%region_8.8_spmd, %region_9.9_spmd} | conditional | flops 809502720 | bytes 36605924 | solution.py:166
  185.5 1.6 copy.25
  192.6 1.4 dynamic-slice_convert_fusion.3
  194.0 1.7 sine_negate_fusion.9
  195.7 9.4 %conditional.9 = ((f32[256,1024]{1,0:T(8,128)}, f32[256,1024]{1,0:T(8,128)}, f32[1024]{0:T(1024)S(1)})) conditional(s32[]{:T(128)} %convert_element_type.321, (f32[256,1024]{1,0:T(8,128)}, f32[256,1024]{1,0:T(8,128)}, f32[1024]{0:T(1024)S(1)}) %tuple.96, (s32[]{:T(128)}, s32[]{:T(128)}, f32[4,64,256]{2,1,0:T(8,128)}, f32[256,256]{1,0:T(8,128)}, ...), branch_computations={%region_8.8_spmd, %region_9.9_spmd} | conditional | flops 809502720 | bytes 36605924 | solution.py:166
  198.1 1.6 copy.25
  205.2 2.9 fusion.52
  208.1 1.6 fusion.23
  210.9 13.4 %all_to_all.111 = bf16[8,32,1024]{2,1,0:T(8,128)(2,1)S(1)} all-to-all(bf16[8,32,1024]{2,1,0:T(8,128)(2,1)S(1)} %bitcast.147), channel_id=1, replica_groups=mesh['ctx'=4,'ch'=8] {'ch'}, dimensions={0} | all-to-all | bytes 1048576 | tf_op jit(solution)/shard_map/all_to_all | solution.py:219
  224.4 3.6 %all-to-all-start.6 = ((bf16[8,32,1024]{2,1,0:T(8,128)(2,1)}), bf16[8,32,1024]{2,1,0:T(8,128)(2,1)S(1)}, u32[]{:S(2)}, u32[]{:S(2)}) async-start(bf16[8,32,1024]{2,1,0:T(8,128)(2,1)} %bitcast.48), calls=%async_computation.6 | async-start | bytes 1048576 | tf_op jit(solution)/shard_map/all_to_all | solution.py:220
  228.2 2.9 fusion.34
  231.1 3.0 fusion.22
  234.1 60.3 %psum.23 = f32[4,64]{1,0:T(4,128)S(1)} all-reduce(f32[4,64]{1,0:T(4,128)S(1)} %get-tuple-element.559), channel_id=1, replica_groups=mesh['ctx'=4,'ch'=8] {'ctx'}, use_global_device_ids=true, to_apply=%region_13.14 | all-reduce | flops 256 | bytes 2048 | tf_op jit(solution)/shard_map/psum | solution.py:180
  295.5 5.4 %all-to-all-start.4 = ((bf16[8,32,1024]{2,1,0:T(8,128)(2,1)}), bf16[8,32,1024]{2,1,0:T(8,128)(2,1)S(1)}, u32[]{:S(2)}, u32[]{:S(2)}) async-start(bf16[8,32,1024]{2,1,0:T(8,128)(2,1)} %bitcast.42), calls=%async_computation.4 | async-start | bytes 1048576 | tf_op jit(solution)/shard_map/all_to_all | solution.py:218
  300.9 20.7 %all-reduce.4.cloned.1.call-done = (f32[4,64,256]{2,1,0:T(8,128)}, f32[4,64,256]{2,1,0:T(8,128)}) async-done(((f32[4,64,256]{2,1,0:T(8,128)}, f32[4,64,256]{2,1,0:T(8,128)}), (f32[4,64,256]{2,1,0:T(8,128)}, f32[4,64,256]{2,1,0:T(8,128)})) %all-reduce.4.cloned.1.call-update) | async-done | bytes 524304 | tf_op jit(solution)/shard_map/psum | solution.py:180
  321.5 2.1 fusion.48
  323.6 2.1 fusion.50
  326.9 1.9 fusion.26
  (194 shorter events, 63.1 us)
Async XLA Ops:
  7.2 9.3 %copy-start.16 = (bf16[32,8192]{1,0:T(8,128)(2,1)S(1)}, bf16[32,8192]{1,0:T(8,128)(2,1)}, u32[]{:S(2)}) copy-start(bf16[32,8192]{1,0:T(8,128)(2,1)} %param.17) | copy-start | bytes 1572868
  9.1 21.8 %all-to-all-start = ((bf16[32,8,1024]{2,0,1:T(8,128)(2,1)}), bf16[32,8,1024]{2,0,1:T(8,128)(2,1)S(1)}, u32[]{:S(2)}, u32[]{:S(2)}) async-start(bf16[32,8,1024]{2,0,1:T(8,128)(2,1)} %bitcast.141), calls=%async_computation | async-start | bytes 1048576 | tf_op jit(solution)/shard_map/all_to_all | solution.py:200
  16.4 105.9 %all-gather.8.cloned.1.call-start = ((), (), s32[]{:S(2)}) async-start(), calls=%async_computation.8 | async-start | bytes 2621440 | tf_op jit(solution)/shard_map/all_gather | solution.py:150
  16.4 33.5 %copy-start.17 = (bf16[32,8192]{1,0:T(8,128)(2,1)S(1)}, bf16[32,8192]{1,0:T(8,128)(2,1)}, u32[]{:S(2)}) copy-start(bf16[32,8192]{1,0:T(8,128)(2,1)} %param.18) | copy-start | bytes 1572868
  30.9 20.0 %copy-start.9 = (bf16[32,8,1024]{2,0,1:T(8,128)(2,1)}, bf16[32,8,1024]{2,0,1:T(8,128)(2,1)S(1)}, u32[]{:S(2)}) copy-start(bf16[32,8,1024]{2,0,1:T(8,128)(2,1)S(1)} %all-to-all-done) | copy-start | bytes 1572868
  49.0 5.5 %copy-start.18 = (bf16[32,8192]{1,0:T(8,128)(2,1)S(1)}, bf16[32,8192]{1,0:T(8,128)(2,1)}, u32[]{:S(2)}) copy-start(bf16[32,8192]{1,0:T(8,128)(2,1)} %param.19) | copy-start | bytes 1572868
  50.8 17.8 %all-to-all-start.1 = ((bf16[32,8,1024]{2,0,1:T(8,128)(2,1)}), bf16[32,8,1024]{2,0,1:T(8,128)(2,1)S(1)}, u32[]{:S(2)}, u32[]{:S(2)}) async-start(bf16[32,8,1024]{2,0,1:T(8,128)(2,1)} %bitcast.140), calls=%async_computation.1 | async-start | bytes 1048576 | tf_op jit(solution)/shard_map/all_to_all | solution.py:198
  54.5 67.9 %all-gather.6.cloned.1.call-start = ((), (), s32[]{:S(2)}) async-start(), calls=%async_computation.7 | async-start | bytes 2621440 | tf_op jit(solution)/shard_map/all_gather | solution.py:149
  54.5 33.9 %copy-start.19 = (f32[64,256]{1,0:T(8,128)S(1)}, f32[64,256]{1,0:T(8,128)}, u32[]{:S(2)}) copy-start(f32[64,256]{1,0:T(8,128)} %param.21) | copy-start | bytes 196612
  54.5 35.3 %copy-start.23 = (u32[32]{0:T(128)S(1)}, u32[32]{0:T(128)}, u32[]{:S(2)}) copy-start(u32[32]{0:T(128)} %constant.195) | copy-start | bytes 388
  68.7 32.5 %copy-start.11 = (bf16[32,8,1024]{2,0,1:T(8,128)(2,1)}, bf16[32,8,1024]{2,0,1:T(8,128)(2,1)S(1)}, u32[]{:S(2)}) copy-start(bf16[32,8,1024]{2,0,1:T(8,128)(2,1)S(1)} %all-to-all-done.1) | copy-start | bytes 1572868
  86.6 0.8 copy-start.13
  88.4 28.9 %copy-start.15 = (bf16[256,1024]{1,0:T(8,128)(2,1)S(1)}, bf16[256,1024]{1,0:T(8,128)(2,1)}, u32[]{:S(2)}) copy-start(bf16[256,1024]{1,0:T(8,128)(2,1)} %fusion.30) | copy-start | bytes 1572868
  88.4 2.7 collective-permute-start
  139.4 1.7 copy-start.1
  139.4 1.7 copy-start.8
  146.3 4.1 %copy-start = (f32[256,1024]{1,0:T(8,128)S(1)}, f32[256,1024]{1,0:T(8,128)}, u32[]{:S(2)}) copy-start(f32[256,1024]{1,0:T(8,128)} %get-tuple-element.736) | copy-start | bytes 3145732 | tf_op jit(solution)/shard_map/while/body/eval_jaxpr/cond
  148.9 4.2 %copy-start.21 = (s32[3]{0:T(128)S(1)}, s32[3]{0:T(128)}, u32[]{:S(2)}) copy-start(s32[3]{0:T(128)} %constant.169.clone) | copy-start | bytes 40 | tf_op jit(solution)/shard_map/while/body/eval_jaxpr/cond
  150.3 6.3 %copy-start.20 = (s32[2]{0:T(128)S(1)}, s32[2]{0:T(128)}, u32[]{:S(2)}) copy-start(s32[2]{0:T(128)} %constant.172.clone) | copy-start | bytes 28 | tf_op jit(solution)/shard_map/while/body/eval_jaxpr/cond
  161.9 1.0 copy-start.2
  161.9 1.3 copy-start.3
  161.9 1.6 copy-start.6
  164.8 1.0 copy-start.4
  165.8 1.0 copy-start.7
  174.5 1.0 copy-start.2
  174.5 1.3 copy-start.3
  174.5 1.6 copy-start.6
  177.4 1.0 copy-start.4
  178.4 1.0 copy-start.7
  187.1 1.0 copy-start.2
  187.1 1.3 copy-start.3
  187.1 1.6 copy-start.6
  190.0 1.0 copy-start.4
  191.0 1.0 copy-start.7
  199.7 1.0 copy-start.2
  199.7 1.3 copy-start.3
  199.7 1.6 copy-start.6
  202.6 1.0 copy-start.4
  203.6 1.0 copy-start.7
  205.1 3.0 copy-start.5
  205.1 4.6 %copy-start.12 = (bf16[32,8,1024]{2,0,1:T(8,128)(2,1)S(1)}, bf16[32,8,1024]{2,0,1:T(8,128)(2,1)}, u32[]{:S(2)}) copy-start(bf16[32,8,1024]{2,0,1:T(8,128)(2,1)} %copy-done.11) | copy-start | bytes 1572868
  205.2 4.6 %copy-start.14 = (bf16[32,8,1024]{2,0,1:T(8,128)(2,1)S(1)}, bf16[32,8,1024]{2,0,1:T(8,128)(2,1)}, u32[]{:S(2)}) copy-start(bf16[32,8,1024]{2,0,1:T(8,128)(2,1)} %copy-done.13) | copy-start | bytes 1572868
  224.4 71.1 %all-to-all-start.6 = ((bf16[8,32,1024]{2,1,0:T(8,128)(2,1)}), bf16[8,32,1024]{2,1,0:T(8,128)(2,1)S(1)}, u32[]{:S(2)}, u32[]{:S(2)}) async-start(bf16[8,32,1024]{2,1,0:T(8,128)(2,1)} %bitcast.48), calls=%async_computation.6 | async-start | bytes 1048576 | tf_op jit(solution)/shard_map/all_to_all | solution.py:220
  227.9 93.6 %all-reduce.4.cloned.1.call-start = ((), (), s32[]{:S(2)}) async-start(), calls=%async_computation.9 | async-start | bytes 1048576 | tf_op jit(solution)/shard_map/psum | solution.py:180
  231.1 63.4 %copy-start.10 = (bf16[32,8,1024]{2,0,1:T(8,128)(2,1)S(1)}, bf16[32,8,1024]{2,0,1:T(8,128)(2,1)}, u32[]{:S(2)}) copy-start(bf16[32,8,1024]{2,0,1:T(8,128)(2,1)} %copy-done.9) | copy-start | bytes 1572868
  295.5 35.0 %all-to-all-start.4 = ((bf16[8,32,1024]{2,1,0:T(8,128)(2,1)}), bf16[8,32,1024]{2,1,0:T(8,128)(2,1)S(1)}, u32[]{:S(2)}, u32[]{:S(2)}) async-start(bf16[8,32,1024]{2,1,0:T(8,128)(2,1)} %bitcast.42), calls=%async_computation.4 | async-start | bytes 1048576 | tf_op jit(solution)/shard_map/all_to_all | solution.py:218
  321.5 4.2 %copy-start.22 = (f32[4,64,256]{2,1,0:T(8,128)S(1)}, f32[4,64,256]{2,1,0:T(8,128)}, u32[]{:S(2)}) copy-start(f32[4,64,256]{2,1,0:T(8,128)} %get-tuple-element.734) | copy-start | bytes 786436
Sparse Core Ops, SparseCore 0:
  50.1 21.6 all-gather.7
  88.5 23.1 all-gather.5
  234.3 87.2 all-reduce.3
where the time goes:
time: 340 us; the launch traced here: 338 us
  blocking collectives  133 us (39%)
  local copies, waits for them, and re-layouts  53.2 us (16%)
  waiting for transfers between devices  49.1 us (14%)
  matrix products  41.7 us (12%)
  other arithmetic  24.1 us (7%)
  starting transfers between devices  21.6 us (6%)
  between operations  14.7 us (4%)
    psum x1, blocking collectives, by_blocks(): total_re, total_im, total_ny = lax.psum((corr_re, corr_im, corr_ny), 'ctx')  60.3 us
    psum x1, waiting for transfers between devices, by_blocks(): total_re, total_im, total_ny = lax.psum((corr_re, corr_im, corr_ny), 'ctx')  20.7 us
    all_to_all x1, blocking collectives, on_device(): lax.all_to_all(query_gate, 'ch', split_axis=1, concat_axis=0, tiled=True)  18.1 us
    all_to_all x1, blocking collectives, on_device(): lax.all_to_all(value_proj, 'ch', split_axis=1, concat_axis=0, tiled=True)  17.9 us
    all_to_all x1, waiting for transfers between devices, on_device(): lax.all_to_all(grad_out, 'ch', split_axis=1, concat_axis=0, tiled=True)  14.4 us
    all_to_all x1, waiting for transfers between devices, on_device(): lax.all_to_all(key_gate, 'ch', split_axis=1, concat_axis=0, tiled=True)  14.1 us
    all_to_all x1, blocking collectives, on_device(): lax.all_to_all(grad_key, 'ch', split_axis=0, concat_axis=1, tiled=True)  13.4 us
    cond x50, local copies, waits for them, and re-layouts  12 us
  transfers between devices with their start and end apart: 8, of which 3 were waited for; matrix products, arithmetic and copies ran while one was open for 8% of the time, Pallas kernels for 0%

commit v1 on v0

--- a/solution.py
+++ b/solution.py
@@ -1,8 +1,11 @@
+import functools
 import math
 
 import jax
 import jax.numpy as jnp
 from jax import lax
+from jax.experimental import pallas as pl
+from jax.experimental.pallas import tpu as pltpu
 from jax.sharding import PartitionSpec as P
 
 GROUP_CH = 16
@@ -222,7 +225,354 @@
     return (query_rows, key_rows, value_rows, grad_filters)
 
 
+TAPS_BLOCK = 128
+CHUNK_CH = 128
+MESH = pl.DeviceIdType.MESH
+NT = (((1,), (1,)), ((), ()))
+
+
+def exchange_kernel(
+    nctx, nch, chunks,
+    query_ref, key_ref, value_ref, grad_ref, taps_ref,
+    out_ref, filt_ref,
+    staged, landed, back, taps, sums, xt, ut, yt, zt,
+    in_send, in_recv, out_send, out_recv, tap_send, tap_recv, sum_send, sum_recv, local_sem,
+):
+    ctx = lax.axis_index("ctx")
+    ch = lax.axis_index("ch")
+    ndev = nctx * nch
+    me = ctx * nch + ch
+    tokens = query_ref.shape[0]
+    chans = query_ref.shape[1] // ndev
+    groups = chans // GROUP_CH
+    span = taps_ref.shape[1]
+    seq = tokens * ndev
+    block = TAPS_BLOCK
+    nblocks = seq // block
+    per_block = block // tokens
+    chunk_groups = CHUNK_CH // GROUP_CH
+
+    def partner(n):
+        order = n // nctx
+        step = (order % 2) * (0 - (order + 1) // 2) + (1 - order % 2) * (order // 2)
+        other_ch = (ch + nch // 2 + step + nch) % nch
+        other_ctx = (ctx + n + 1) % nctx
+        return other_ctx, other_ch
+
+    def columns(owner_ctx, owner_ch, chunk):
+        start = owner_ch * (nctx * chans) + owner_ctx * chans + chunk * CHUNK_CH
+        return pl.ds(pl.multiple_of(start, 128), CHUNK_CH)
+
+    def gate(cols):
+        staged[0:tokens, cols] = (
+            key_ref[:, cols].astype(jnp.float32) * value_ref[:, cols].astype(jnp.float32)
+        ).astype(jnp.bfloat16)
+        staged[tokens:, cols] = (
+            grad_ref[:, cols].astype(jnp.float32) * query_ref[:, cols].astype(jnp.float32)
+        ).astype(jnp.bfloat16)
+
+    def in_copy(chunk, n):
+        other_ctx, other_ch = partner(n)
+        return pltpu.make_async_remote_copy(
+            src_ref=staged.at[:, columns(other_ctx, other_ch, chunk)],
+            dst_ref=landed.at[chunk, me],
+            send_sem=in_send.at[chunk, n],
+            recv_sem=in_recv.at[chunk, me],
+            device_id=(other_ctx, other_ch),
+            device_id_type=MESH,
+        )
+
+    def in_arrival(chunk, n):
+        other_ctx, other_ch = partner(n)
+        other = other_ctx * nch + other_ch
+        return pltpu.make_async_remote_copy(
+            src_ref=staged.at[:, columns(other_ctx, other_ch, chunk)],
+            dst_ref=landed.at[chunk, other],
+            send_sem=in_send.at[chunk, n],
+            recv_sem=in_recv.at[chunk, other],
+            device_id=(other_ctx, other_ch),
+            device_id_type=MESH,
+        )
+
+    def out_copy(chunk, n):
+        other_ctx, other_ch = partner(n)
+        other = other_ctx * nch + other_ch
+        return pltpu.make_async_remote_copy(
+            src_ref=back.at[chunk, other],
+            dst_ref=out_ref.at[:, columns(ctx, ch, chunk)],
+            send_sem=out_send.at[chunk, n],
+            recv_sem=out_recv.at[chunk, me],
+            device_id=(other_ctx, other_ch),
+            device_id_type=MESH,
+        )
+
+    def out_arrival(chunk, n):
+        other_ctx, other_ch = partner(n)
+        other = other_ctx * nch + other_ch
+        return pltpu.make_async_remote_copy(
+            src_ref=back.at[chunk, other],
+            dst_ref=out_ref.at[:, columns(other_ctx, other_ch, chunk)],
+            send_sem=out_send.at[chunk, n],
+            recv_sem=out_recv.at[chunk, other],
+            device_id=(other_ctx, other_ch),
+            device_id_type=MESH,
+        )
+
+    def tap_copy(step, sender):
+        other = (ctx + step) % nctx
+        slot = ctx if sender else other
+        return pltpu.make_async_remote_copy(
+            src_ref=taps_ref.at[pl.ds(pl.multiple_of(other * groups, 8), groups), :],
+            dst_ref=taps.at[:, pl.ds(pl.multiple_of(slot * span, 128), span)],
+            send_sem=tap_send.at[step],
+            recv_sem=tap_recv.at[slot],
+            device_id=(other, ch),
+            device_id_type=MESH,
+        )
+
+    def sum_copy(step, sender):
+        other = (ctx + step) % nctx
+        slot = ctx if sender else other
+        return pltpu.make_async_remote_copy(
+            src_ref=sums.at[:, pl.ds(pl.multiple_of(other * span, 128), span)],
+            dst_ref=filt_ref.at[pl.ds(pl.multiple_of(slot * groups, 8), groups), :],
+            send_sem=sum_send.at[step],
+            recv_sem=sum_recv.at[slot],
+            device_id=(other, ch),
+            device_id_type=MESH,
+        )
+
+    def own_in(chunk):
+        return pltpu.make_async_copy(
+            staged.at[:, columns(ctx, ch, chunk)], landed.at[chunk, me], local_sem.at[chunk]
+        )
+
+    def own_out(chunk):
+        return pltpu.make_async_copy(
+            back.at[chunk, me], out_ref.at[:, columns(ctx, ch, chunk)], local_sem.at[chunks + chunk]
+        )
+
+    def each(count, body):
+        def step(n, carry):
+            body(n)
+            return carry
+
+        lax.fori_loop(0, count, step, 0)
+
+    barrier = pltpu.get_barrier_semaphore()
+
+    def greet(n):
+        other_ctx, other_ch = partner(n)
+        pl.semaphore_signal(barrier, inc=1, device_id=(other_ctx, other_ch), device_id_type=MESH)
+
+    each(ndev - 1, greet)
+
+    def gate_chunk(chunk):
+        each(
+            ndev,
+            lambda n: gate(pl.ds(pl.multiple_of(n * chans + chunk * CHUNK_CH, 128), CHUNK_CH)),
+        )
+
+    gate_chunk(0)
+    pl.semaphore_wait(barrier, ndev - 1)
+    each(ndev - 1, lambda n: in_copy(0, n).start())
+    for step in range(1, nctx):
+        tap_copy(step, True).start()
+    own_in(0).start()
+    own_taps = pltpu.make_async_copy(
+        taps_ref.at[pl.ds(pl.multiple_of(ctx * groups, 8), groups), :],
+        taps.at[:, pl.ds(pl.multiple_of(ctx * span, 128), span)],
+        local_sem.at[2 * chunks],
+    )
+    own_taps.start()
+    for chunk in range(1, chunks):
+        gate_chunk(chunk)
+        each(ndev - 1, lambda n: in_copy(chunk, n).start())
+        own_in(chunk).start()
+    own_taps.wait()
+    for step in range(1, nctx):
+        tap_copy(step, False).wait_recv()
+
+    row_id = lax.broadcasted_iota(jnp.int32, (block, block), 0)
+    col_id = lax.broadcasted_iota(jnp.int32, (block, block), 1)
+    flip = (row_id + col_id == block - 1).astype(jnp.bfloat16)
+    zeros = jnp.zeros((block, block), jnp.bfloat16)
+    width = block + seq
+
+    def slide(values, shift):
+        return pltpu.roll(values, shift, 1, stride=1, stride_axis=0)[:, block:]
+
+    def later(stack):
+        padded = jnp.concatenate([stack, zeros], axis=0)
+        return jnp.concatenate(
+            [padded[k * GROUP_CH : k * GROUP_CH + block] for k in range(nblocks)], axis=1
+        )
+
+    def earlier(stack):
+        padded = jnp.concatenate([zeros, stack], axis=0)
+        return jnp.concatenate(
+            [padded[block - k * GROUP_CH : 2 * block - k * GROUP_CH] for k in range(nblocks)],
+            axis=1,
+        )
+
+    def turn_in(chunk):
+        for i in range(nblocks):
+            src = pl.ds(i * per_block, per_block)
+            for rows, dst in ((pl.ds(0, tokens), xt), (pl.ds(tokens, tokens), ut)):
+                tile = landed[chunk, src, rows, :].reshape(block, CHUNK_CH)
+                dst[:, i] = tile.T.reshape(chunk_groups, GROUP_CH, block)
+
+    def convolve(chunk, g):
+        stack_x = xt[g].reshape(block, block)
+        stack_u = ut[g].reshape(block, block)
+        row = taps[pl.ds(chunk * chunk_groups + g, 1), :]
+        row = jnp.concatenate([jnp.zeros((1, block), jnp.float32), row], axis=1)
+        wide = slide(jnp.broadcast_to(row, (block, width)), 0)
+        high = wide.astype(jnp.bfloat16)
+        low = (wide - high.astype(jnp.float32)).astype(jnp.bfloat16)
+        x_cat = earlier(stack_x)
+        u_cat = later(stack_u)
+        conv = jnp.zeros((block, block), jnp.float32)
+        corr = jnp.zeros((block, block), jnp.float32)
+        for part in (high, low):
+            tall = jnp.concatenate(
+                [part[:, k * block : (k + 1) * block] for k in range(nblocks)], axis=0
+            )
+            conv = conv + jnp.dot(x_cat, tall, preferred_element_type=jnp.float32)
+            corr = corr + lax.dot_general(u_cat, part, NT, preferred_element_type=jnp.float32)
+        yt[:, pl.ds(pl.multiple_of(g * GROUP_CH, GROUP_CH), GROUP_CH), :] = (
+            conv.astype(jnp.bfloat16).reshape(nblocks, GROUP_CH, block)
+        )
+        zt[:, pl.ds(pl.multiple_of(g * GROUP_CH, GROUP_CH), GROUP_CH), :] = (
+            corr.astype(jnp.bfloat16).reshape(nblocks, GROUP_CH, block)
+        )
+
+    def turn_out(chunk):
+        for i in range(nblocks):
+            dst = pl.ds(i * per_block, per_block)
+            back[chunk, dst, 0:tokens, :] = yt[i].T.reshape(per_block, tokens, CHUNK_CH)
+            back[chunk, dst, tokens:, :] = zt[i].T.reshape(per_block, tokens, CHUNK_CH)
+
+    def correlate(chunk, g):
+        stack_x = xt[g].reshape(block, block)
+        u_cat = later(ut[g].reshape(block, block))
+        turned = lax.dot_general(
+            flip, stack_x, NT, preferred_element_type=jnp.float32
+        ).astype(jnp.bfloat16)
+        pairs = jnp.dot(turned, u_cat, preferred_element_type=jnp.float32)
+        pairs = jnp.concatenate([pairs, jnp.zeros((block, block), jnp.float32)], axis=1)
+        total = jnp.sum(slide(pairs, 1), axis=0, keepdims=True)
+        sums[pl.ds(chunk * chunk_groups + g, 1), :] = total
+
+    for chunk in range(chunks):
+        own_in(chunk).wait()
+        each(ndev - 1, lambda n: in_arrival(chunk, n).wait_recv())
+        turn_in(chunk)
+        each(chunk_groups, lambda g: convolve(chunk, g))
+        turn_out(chunk)
+        each(ndev - 1, lambda n: out_copy(chunk, n).start())
+        own_out(chunk).start()
+        each(chunk_groups, lambda g: correlate(chunk, g))
+
+    for step in range(1, nctx):
+        sum_copy(step, True).start()
+    own_sums = pltpu.make_async_copy(
+        sums.at[:, pl.ds(pl.multiple_of(ctx * span, 128), span)],
+        filt_ref.at[pl.ds(pl.multiple_of(ctx * groups, 8), groups), :],
+        local_sem.at[2 * chunks + 1],
+    )
+    own_sums.start()
+
+    for step in range(1, nctx):
+        tap_copy(step, True).wait_send()
+    for chunk in range(chunks):
+        each(ndev - 1, lambda n: in_copy(chunk, n).wait_send())
+        each(ndev - 1, lambda n: out_copy(chunk, n).wait_send())
+        each(ndev - 1, lambda n: out_arrival(chunk, n).wait_recv())
+        own_out(chunk).wait()
+    for step in range(1, nctx):
+        sum_copy(step, True).wait_send()
+        sum_copy(step, False).wait_recv()
+    own_sums.wait()
+
+
+def one_exchange(nctx, nch, query_gate, key_gate, value_proj, grad_out, long_filters):
+    tokens, model = query_gate.shape
+    ndev = nctx * nch
+    chans = model // ndev
+    groups = chans // GROUP_CH
+    chunks = chans // CHUNK_CH
+    seq = tokens * ndev
+    nblocks = seq // TAPS_BLOCK
+    chunk_groups = CHUNK_CH // GROUP_CH
+    vmem = pl.BlockSpec(memory_space=pltpu.VMEM)
+    half = jnp.bfloat16
+    sem = pltpu.SemaphoreType.DMA
+    returned, grad_filters = pl.pallas_call(
+        functools.partial(exchange_kernel, nctx, nch, chunks),
+        out_shape=(
+            jax.ShapeDtypeStruct((2 * tokens, model), half),
+            jax.ShapeDtypeStruct(long_filters.shape, jnp.float32),
+        ),
+        in_specs=[vmem] * 5,
+        out_specs=(vmem, vmem),
+        scratch_shapes=[
+            pltpu.VMEM((2 * tokens, model), half),
+            pltpu.VMEM((chunks, ndev, 2 * tokens, CHUNK_CH), half),
+            pltpu.VMEM((chunks, ndev, 2 * tokens, CHUNK_CH), half),
+            pltpu.VMEM((groups, seq), jnp.float32),
+            pltpu.VMEM((groups, seq), jnp.float32),
+            pltpu.VMEM((chunk_groups, nblocks, GROUP_CH, TAPS_BLOCK), half),
+            pltpu.VMEM((chunk_groups, nblocks, GROUP_CH, TAPS_BLOCK), half),
+            pltpu.VMEM((nblocks, CHUNK_CH, TAPS_BLOCK), half),
+            pltpu.VMEM((nblocks, CHUNK_CH, TAPS_BLOCK), half),
+            sem((chunks, ndev)),
+            sem((chunks, ndev)),
+            sem((chunks, ndev)),
+            sem((chunks, ndev)),
+            sem((nctx,)),
+            sem((nctx,)),
+            sem((nctx,)),
+            sem((nctx,)),
+            sem((2 * chunks + 2,)),
+        ],
+        compiler_params=pltpu.CompilerParams(
+            collective_id=0, has_side_effects=True, vmem_limit_bytes=40 * 1024 * 1024
+        ),
+        name="exchange_and_convolve",
+    )(query_gate, key_gate, value_proj, grad_out, long_filters)
+    convolved = returned[:tokens].astype(jnp.float32)
+    correlated = returned[tokens:].astype(jnp.float32)
+    return (
+        (grad_out.astype(jnp.float32) * convolved).astype(half),
+        (correlated * value_proj.astype(jnp.float32)).astype(half),
+        (correlated * key_gate.astype(jnp.float32)).astype(half),
+        grad_filters,
+    )
+
+
+def fits_one_exchange(nctx, nch, query_shape, filter_shape):
+    tokens, model = query_shape
+    ndev = nctx * nch
+    return (
+        model % (ndev * CHUNK_CH) == 0
+        and tokens % 16 == 0
+        and TAPS_BLOCK % tokens == 0
+        and tokens * ndev == TAPS_BLOCK * (TAPS_BLOCK // GROUP_CH)
+        and filter_shape[1] % 128 == 0
+        and nctx * filter_shape[0] * nch * GROUP_CH == model * nctx
+    )
+
+
 def solution(mesh):
+    nctx, nch = mesh.shape["ctx"], mesh.shape["ch"]
+
+    def local(query_gate, key_gate, value_proj, grad_out, long_filters):
+        args = (query_gate, key_gate, value_proj, grad_out, long_filters)
+        if fits_one_exchange(nctx, nch, query_gate.shape, long_filters.shape):
+            return one_exchange(nctx, nch, *args)
+        return on_device(*args)
+
     in_specs = (
         P(("ctx", "ch"), None),
         P(("ctx", "ch"), None),
@@ -237,5 +587,5 @@
         P("ch", "ctx"),
     )
     return jax.shard_map(
-        on_device, mesh=mesh, in_specs=in_specs, out_specs=out_specs, check_vma=False
-    )
+        local, mesh=mesh, in_specs=in_specs, out_specs=out_specs, check_vma=False
+    )

time: 340 us -> 64.6 us (0.19)
  blocking collectives: 133 us -> 0 us
  Pallas kernels: 0 us -> 56.6 us
  waiting for transfers between devices: 49.1 us -> 0 us
  local copies, waits for them, and re-layouts: 53.2 us -> 5.63 us
  matrix products: 41.7 us -> 0 us
  other arithmetic: 24.1 us -> 1.35 us
  starting transfers between devices: 21.6 us -> 0 us
  between operations: 14.7 us -> 0.65 us
    psum x1 -> x0, blocking collectives: 60.3 us -> none  [by_blocks(): total_re, total_im, total_ny = lax.psum((corr_re, corr_im, corr_ny), 'ctx')]
    pallas_call x0 -> x1, Pallas kernels: none -> 56.6 us  [one_exchange(): pl.pallas_call(functools.partial(exchange_kernel, nctx, nch, chunks), out...]
    all_to_all x3 -> x0, blocking collectives: 49.4 us -> none  [the longest x1 18.1 us: on_device(): lax.all_to_all(query_gate, 'ch', split_axis=1, concat_axis=0, tiled=True)]
    dot_general x29 -> x0, matrix products: 41.7 us -> none  [the longest x6 9.93 us: columns_forward(): jnp.dot(tables[1], values, precision=SPLIT_MODE)]
    all_to_all x4 -> x0, waiting for transfers between devices: 28.4 us -> none  [the longest x1 14.4 us: on_device(): lax.all_to_all(grad_out, 'ch', split_axis=1, concat_axis=0, tiled=True)]
    psum x1 -> x0, waiting for transfers between devices: 20.7 us -> none  [by_blocks(): total_re, total_im, total_ny = lax.psum((corr_re, corr_im, corr_ny), 'ctx')]
    all_to_all x4 -> x0, starting transfers between devices: 19.9 us -> none  [the longest x1 7.28 us: on_device(): lax.all_to_all(grad_out, 'ch', split_axis=1, concat_axis=0, tiled=True)]
    all_gather x2 -> x0, blocking collectives: 14.8 us -> none  [the longest x1 8.47 us: by_blocks(): lax.all_gather(own_re[None], 'ctx', axis=0, tiled=True)]
  transfers between devices with their start and end apart: 8 -> 0, of which waited for: 3 -> 0; matrix products, arithmetic and copies ran while one was open for 8% -> 0% of each run, Pallas kernels for 0% -> 0%
where the time goes in v1:
time: 64.6 us; the launch traced here: 64.2 us
  Pallas kernels  56.6 us (88%)
  local copies, waits for them, and re-layouts  5.63 us (9%)
  other arithmetic  1.35 us (2%)
  between operations  0.65 us (1%)
    pallas_call x1, Pallas kernels, one_exchange(): pl.pallas_call(functools.partial(exchange_kernel, nctx, nch, chunks), out...  56.6 us
    unnamed x11, local copies, waits for them, and re-layouts  5.63 us
    convert_element_type x1, other arithmetic, one_exchange(): (correlated * key_gate.astype(jnp.float32)).astype(half)  1.35 us

profile of v1, /device:TPU:0, one launch (start us, length us, event | category | flops | bytes accessed | tf_op | source)
XLA Modules:
  0.0 64.2 jit_solution(308315197027933321)
XLA Ops:
  0.6 0.0 copy-start
  0.6 1.0 %copy-done = bf16[32,8192]{1,0:T(8,128)(2,1)S(1)} copy-done((bf16[32,8192]{1,0:T(8,128)(2,1)S(1)}, bf16[32,8192]{1,0:T(8,128)(2,1)}, u32[]{:S(2)}) %copy-start) | copy-done | bytes 524312
  1.7 0.0 copy-start.1
  1.7 1.0 %copy-done.1 = bf16[32,8192]{1,0:T(8,128)(2,1)S(1)} copy-done((bf16[32,8192]{1,0:T(8,128)(2,1)S(1)}, bf16[32,8192]{1,0:T(8,128)(2,1)}, u32[]{:S(2)}) %copy-start.1) | copy-done | bytes 524312
  2.7 0.0 copy-start.2
  2.7 1.0 %copy-done.2 = bf16[32,8192]{1,0:T(8,128)(2,1)S(1)} copy-done((bf16[32,8192]{1,0:T(8,128)(2,1)S(1)}, bf16[32,8192]{1,0:T(8,128)(2,1)}, u32[]{:S(2)}) %copy-start.2) | copy-done | bytes 524312
  3.8 0.0 copy-start.3
  3.8 1.0 %copy-done.3 = bf16[32,8192]{1,0:T(8,128)(2,1)S(1)} copy-done((bf16[32,8192]{1,0:T(8,128)(2,1)S(1)}, bf16[32,8192]{1,0:T(8,128)(2,1)}, u32[]{:S(2)}) %copy-start.3) | copy-done | bytes 524312
  4.8 0.0 copy-start.4
  4.8 0.8 %copy-done.4 = f32[64,256]{1,0:T(8,128)S(1)} copy-done((f32[64,256]{1,0:T(8,128)S(1)}, f32[64,256]{1,0:T(8,128)}, u32[]{:S(2)}) %copy-start.4) | copy-done | bytes 65560
  5.6 56.6 %exchange_and_convolve.1 = (bf16[64,8192]{1,0:T(8,128)(2,1)S(1)}, f32[64,256]{1,0:T(8,128)S(1)}) custom-call(bf16[32,8192]{1,0:T(8,128)(2,1)S(1)} %copy-done.3, bf16[32,8192]{1,0:T(8,128)(2,1)S(1)} %copy-done, bf16[32,8192]{1,0:T(8,128)(2,1)S(1)} %copy-done.1, bf16[32,8192]{1,0:T(8,128)(2,1)S(1)} %copy-done.2, f32[64,256]{1,0:T(8,128)S(1)} %copy-done.4), custom_call_target="tpu_custom_call" | custom-call | tf_op jit(solution)/shard_map/exchange_and_convolve/pallas_call | solution.py:511
  62.2 1.4 %fusion.1 = (bf16[32,8192]{1,0:T(8,128)(2,1)}, bf16[32,8192]{1,0:T(8,128)(2,1)}, bf16[32,8192]{1,0:T(8,128)(2,1)}) fusion(bf16[32,8192]{1,0:T(8,128)(2,1)S(1)} %copy-done, bf16[64,8192]{1,0:T(8,128)(2,1)S(1)} %get-tuple-element.6, bf16[32,8192]{1,0:T(8,128)(2,1)S(1)} %copy-done.1, bf16[32,8192]{1,0:T(8,128)(2,1)S(1)} %copy-done.2), kind=kLoop, calls=%fused_computation.3 | loop fusion | flops 2883584 | bytes 4194304 | tf_op jit(solution)/shard_map/convert_element_type | solution.py:549
  63.6 0.6 copy.10
Async XLA Ops:
  0.6 1.0 %copy-start = (bf16[32,8192]{1,0:T(8,128)(2,1)S(1)}, bf16[32,8192]{1,0:T(8,128)(2,1)}, u32[]{:S(2)}) copy-start(bf16[32,8192]{1,0:T(8,128)(2,1)} %key_ref.1) | copy-start | bytes 1572868
  1.7 1.0 %copy-start.1 = (bf16[32,8192]{1,0:T(8,128)(2,1)S(1)}, bf16[32,8192]{1,0:T(8,128)(2,1)}, u32[]{:S(2)}) copy-start(bf16[32,8192]{1,0:T(8,128)(2,1)} %value_ref.1) | copy-start | bytes 1572868
  2.7 1.0 %copy-start.2 = (bf16[32,8192]{1,0:T(8,128)(2,1)S(1)}, bf16[32,8192]{1,0:T(8,128)(2,1)}, u32[]{:S(2)}) copy-start(bf16[32,8192]{1,0:T(8,128)(2,1)} %grad_ref.1) | copy-start | bytes 1572868
  3.8 1.0 %copy-start.3 = (bf16[32,8192]{1,0:T(8,128)(2,1)S(1)}, bf16[32,8192]{1,0:T(8,128)(2,1)}, u32[]{:S(2)}) copy-start(bf16[32,8192]{1,0:T(8,128)(2,1)} %query_ref.1) | copy-start | bytes 1572868
  4.8 0.8 %copy-start.4 = (f32[64,256]{1,0:T(8,128)S(1)}, f32[64,256]{1,0:T(8,128)}, u32[]{:S(2)}) copy-start(f32[64,256]{1,0:T(8,128)} %taps_ref.1) | copy-start | bytes 196612

commit v2 on v1

--- a/solution.py
+++ b/solution.py
@@ -227,16 +227,17 @@
 
 TAPS_BLOCK = 128
 CHUNK_CH = 128
+LOAD_PIECES = 4
 MESH = pl.DeviceIdType.MESH
 NT = (((1,), (1,)), ((), ()))
 
 
 def exchange_kernel(
     nctx, nch, chunks,
-    query_ref, key_ref, value_ref, grad_ref, taps_ref,
+    query_hbm, key_hbm, value_hbm, grad_hbm, taps_ref,
     out_ref, filt_ref,
-    staged, landed, back, taps, sums, xt, ut, yt, zt,
-    in_send, in_recv, out_send, out_recv, tap_send, tap_recv, sum_send, sum_recv, local_sem,
+    query_ref, key_ref, value_ref, grad_ref, staged, landed, back, taps, sums, toeplitz, xt, ut, yt, zt,
+    in_send, in_recv, out_send, out_recv, tap_send, tap_recv, sum_send, sum_recv, local_sem, load_sem,
 ):
     ctx = lax.axis_index("ctx")
     ch = lax.axis_index("ch")
@@ -352,12 +353,29 @@
             back.at[chunk, me], out_ref.at[:, columns(ctx, ch, chunk)], local_sem.at[chunks + chunk]
         )
 
-    def each(count, body):
+    def each(count, body, unroll=1):
         def step(n, carry):
             body(n)
             return carry
 
-        lax.fori_loop(0, count, step, 0)
+        lax.fori_loop(0, count, step, 0, unroll=unroll)
+
+    pieces = LOAD_PIECES
+    piece = nctx * nch * chans // pieces
+
+    def load(which, part):
+        src, dst = (
+            (query_hbm, query_ref),
+            (key_hbm, key_ref),
+            (value_hbm, value_ref),
+            (grad_hbm, grad_ref),
+        )[which]
+        cols = pl.ds(part * piece, piece)
+        return pltpu.make_async_copy(src.at[:, cols], dst.at[:, cols], load_sem.at[which, part])
+
+    for part in range(pieces):
+        for which in range(4):
+            load(which, part).start()
 
     barrier = pltpu.get_barrier_semaphore()
 
@@ -367,26 +385,32 @@
 
     each(ndev - 1, greet)
 
-    def gate_chunk(chunk):
+    def gate_chunk(chunk, first, count):
         each(
-            ndev,
-            lambda n: gate(pl.ds(pl.multiple_of(n * chans + chunk * CHUNK_CH, 128), CHUNK_CH)),
-        )
-
-    gate_chunk(0)
-    pl.semaphore_wait(barrier, ndev - 1)
-    each(ndev - 1, lambda n: in_copy(0, n).start())
-    for step in range(1, nctx):
-        tap_copy(step, True).start()
-    own_in(0).start()
+            count,
+            lambda n: gate(
+                pl.ds(pl.multiple_of((first + n) * chans + chunk * CHUNK_CH, 128), CHUNK_CH)
+            ),
+            unroll=4,
+        )
+
     own_taps = pltpu.make_async_copy(
         taps_ref.at[pl.ds(pl.multiple_of(ctx * groups, 8), groups), :],
         taps.at[:, pl.ds(pl.multiple_of(ctx * span, 128), span)],
         local_sem.at[2 * chunks],
     )
     own_taps.start()
+    for part in range(pieces):
+        for which in range(4):
+            load(which, part).wait()
+        gate_chunk(0, part * (ndev // pieces), ndev // pieces)
+    pl.semaphore_wait(barrier, ndev - 1)
+    for step in range(1, nctx):
+        tap_copy(step, True).start()
+    each(ndev - 1, lambda n: in_copy(0, n).start())
+    own_in(0).start()
     for chunk in range(1, chunks):
-        gate_chunk(chunk)
+        gate_chunk(chunk, 0, ndev)
         each(ndev - 1, lambda n: in_copy(chunk, n).start())
         own_in(chunk).start()
     own_taps.wait()
@@ -420,26 +444,29 @@
             src = pl.ds(i * per_block, per_block)
             for rows, dst in ((pl.ds(0, tokens), xt), (pl.ds(tokens, tokens), ut)):
                 tile = landed[chunk, src, rows, :].reshape(block, CHUNK_CH)
-                dst[:, i] = tile.T.reshape(chunk_groups, GROUP_CH, block)
-
-    def convolve(chunk, g):
-        stack_x = xt[g].reshape(block, block)
-        stack_u = ut[g].reshape(block, block)
-        row = taps[pl.ds(chunk * chunk_groups + g, 1), :]
+                dst[chunk, :, i] = tile.T.reshape(chunk_groups, GROUP_CH, block)
+
+    def build(group):
+        row = taps[pl.ds(group, 1), :]
         row = jnp.concatenate([jnp.zeros((1, block), jnp.float32), row], axis=1)
         wide = slide(jnp.broadcast_to(row, (block, width)), 0)
         high = wide.astype(jnp.bfloat16)
         low = (wide - high.astype(jnp.float32)).astype(jnp.bfloat16)
-        x_cat = earlier(stack_x)
-        u_cat = later(stack_u)
+        for which, part in ((0, high), (1, low)):
+            for k in range(nblocks):
+                toeplitz[group, which, k] = part[:, k * block : (k + 1) * block]
+
+    def convolve(chunk, g):
+        x_cat = earlier(xt[chunk, g].reshape(block, block))
+        u_cat = later(ut[chunk, g].reshape(block, block))
         conv = jnp.zeros((block, block), jnp.float32)
         corr = jnp.zeros((block, block), jnp.float32)
-        for part in (high, low):
-            tall = jnp.concatenate(
-                [part[:, k * block : (k + 1) * block] for k in range(nblocks)], axis=0
-            )
+        for which in range(2):
+            part = toeplitz[chunk * chunk_groups + g, which]
+            tall = part.reshape(nblocks * block, block)
+            flat = jnp.concatenate([part[k] for k in range(nblocks)], axis=1)
             conv = conv + jnp.dot(x_cat, tall, preferred_element_type=jnp.float32)
-            corr = corr + lax.dot_general(u_cat, part, NT, preferred_element_type=jnp.float32)
+            corr = corr + lax.dot_general(u_cat, flat, NT, preferred_element_type=jnp.float32)
         yt[:, pl.ds(pl.multiple_of(g * GROUP_CH, GROUP_CH), GROUP_CH), :] = (
             conv.astype(jnp.bfloat16).reshape(nblocks, GROUP_CH, block)
         )
@@ -454,8 +481,8 @@
             back[chunk, dst, tokens:, :] = zt[i].T.reshape(per_block, tokens, CHUNK_CH)
 
     def correlate(chunk, g):
-        stack_x = xt[g].reshape(block, block)
-        u_cat = later(ut[g].reshape(block, block))
+        stack_x = xt[chunk, g].reshape(block, block)
+        u_cat = later(ut[chunk, g].reshape(block, block))
         turned = lax.dot_general(
             flip, stack_x, NT, preferred_element_type=jnp.float32
         ).astype(jnp.bfloat16)
@@ -464,15 +491,18 @@
         total = jnp.sum(slide(pairs, 1), axis=0, keepdims=True)
         sums[pl.ds(chunk * chunk_groups + g, 1), :] = total
 
+    each(groups, build, unroll=2)
     for chunk in range(chunks):
         own_in(chunk).wait()
         each(ndev - 1, lambda n: in_arrival(chunk, n).wait_recv())
         turn_in(chunk)
-        each(chunk_groups, lambda g: convolve(chunk, g))
+        each(chunk_groups, lambda g: convolve(chunk, g), unroll=2)
         turn_out(chunk)
         each(ndev - 1, lambda n: out_copy(chunk, n).start())
         own_out(chunk).start()
-        each(chunk_groups, lambda g: correlate(chunk, g))
+
+    for chunk in range(chunks):
+        each(chunk_groups, lambda g: correlate(chunk, g), unroll=2)
 
     for step in range(1, nctx):
         sum_copy(step, True).start()
@@ -514,16 +544,18 @@
             jax.ShapeDtypeStruct((2 * tokens, model), half),
             jax.ShapeDtypeStruct(long_filters.shape, jnp.float32),
         ),
-        in_specs=[vmem] * 5,
+        in_specs=[pl.BlockSpec(memory_space=pltpu.HBM)] * 4 + [vmem],
         out_specs=(vmem, vmem),
-        scratch_shapes=[
+        scratch_shapes=[pltpu.VMEM((tokens, model), half)] * 4
+        + [
             pltpu.VMEM((2 * tokens, model), half),
             pltpu.VMEM((chunks, ndev, 2 * tokens, CHUNK_CH), half),
             pltpu.VMEM((chunks, ndev, 2 * tokens, CHUNK_CH), half),
             pltpu.VMEM((groups, seq), jnp.float32),
             pltpu.VMEM((groups, seq), jnp.float32),
-            pltpu.VMEM((chunk_groups, nblocks, GROUP_CH, TAPS_BLOCK), half),
-            pltpu.VMEM((chunk_groups, nblocks, GROUP_CH, TAPS_BLOCK), half),
+            pltpu.VMEM((groups, 2, nblocks, TAPS_BLOCK, TAPS_BLOCK), half),
+            pltpu.VMEM((chunks, chunk_groups, nblocks, GROUP_CH, TAPS_BLOCK), half),
+            pltpu.VMEM((chunks, chunk_groups, nblocks, GROUP_CH, TAPS_BLOCK), half),
             pltpu.VMEM((nblocks, CHUNK_CH, TAPS_BLOCK), half),
             pltpu.VMEM((nblocks, CHUNK_CH, TAPS_BLOCK), half),
             sem((chunks, ndev)),
@@ -535,9 +567,10 @@
             sem((nctx,)),
             sem((nctx,)),
             sem((2 * chunks + 2,)),
+            sem((4, LOAD_PIECES)),
         ],
         compiler_params=pltpu.CompilerParams(
-            collective_id=0, has_side_effects=True, vmem_limit_bytes=40 * 1024 * 1024
+            collective_id=0, has_side_effects=True, vmem_limit_bytes=56 * 1024 * 1024
         ),
         name="exchange_and_convolve",
     )(query_gate, key_gate, value_proj, grad_out, long_filters)

time: 64.6 us -> 60.7 us (0.940)
  local copies, waits for them, and re-layouts: 5.63 us -> 0.65 us
  other arithmetic: 1.35 us -> 2.58 us
    unnamed x11 -> x9, local copies, waits for them, and re-layouts: 5.63 us -> 0.65 us
    convert_element_type x1, other arithmetic: 1.35 us -> 2.58 us  [one_exchange(): (correlated * key_gate.astype(jnp.float32)).astype(half)]
where the time goes in v2:
time: 60.7 us; the launch traced here: 60.5 us
  Pallas kernels  56.6 us (93%)
  other arithmetic  2.58 us (4%)
  between operations  0.7 us (1%)
  local copies, waits for them, and re-layouts  0.65 us (1%)
    pallas_call x1, Pallas kernels, one_exchange(): pl.pallas_call(functools.partial(exchange_kernel, nctx, nch, chunks), out...  56.6 us
    convert_element_type x1, other arithmetic, one_exchange(): (correlated * key_gate.astype(jnp.float32)).astype(half)  2.58 us

profile of v2, /device:TPU:0, one launch (start us, length us, event | category | flops | bytes accessed | tf_op | source)
XLA Modules:
  0.0 60.5 jit_solution(15267744066263456009)
XLA Ops:
  0.6 0.0 copy-start.2
  0.6 0.0 copy-start.1
  0.7 0.0 copy-start
  0.7 56.6 %exchange_and_convolve.1 = (bf16[64,8192]{1,0:T(8,128)(2,1)}, f32[64,256]{1,0:T(8,128)}) custom-call(bf16[32,8192]{1,0:T(8,128)(2,1)} %query_hbm.1, bf16[32,8192]{1,0:T(8,128)(2,1)} %key_hbm.1, bf16[32,8192]{1,0:T(8,128)(2,1)} %value_hbm.1, bf16[32,8192]{1,0:T(8,128)(2,1)} %grad_hbm.1, f32[64,256]{1,0:T(8,128)} %taps_ref.1), custom_call_target="tpu_custom_call" | custom-call | tf_op jit(solution)/shard_map/exchange_and_convolve/pallas_call | solution.py:541
  57.3 0.0 copy-done.2
  57.3 0.0 copy-done.1
  57.3 0.0 copy-done
  57.3 0.0 copy-start.3
  57.3 2.6 %fusion.1 = (bf16[32,8192]{1,0:T(8,128)(2,1)}, bf16[32,8192]{1,0:T(8,128)(2,1)}, bf16[32,8192]{1,0:T(8,128)(2,1)}) fusion(bf16[32,8192]{1,0:T(8,128)(2,1)S(1)} %copy-done, bf16[64,8192]{1,0:T(8,128)(2,1)} %get-tuple-element.6, bf16[32,8192]{1,0:T(8,128)(2,1)S(1)} %copy-done.1, bf16[32,8192]{1,0:T(8,128)(2,1)S(1)} %copy-done.2), kind=kLoop, calls=%fused_computation.3 | loop fusion | flops 2883584 | bytes 4194304 | tf_op jit(solution)/shard_map/convert_element_type | solution.py:582
  59.9 0.0 copy-done.3
  59.9 0.6 %copy.10 = f32[64,256]{1,0:T(8,128)} copy(f32[64,256]{1,0:T(8,128)S(1)} %copy-done.3) | data formatting | bytes 131072
Async XLA Ops:
  0.6 56.7 %copy-start.2 = (bf16[32,8192]{1,0:T(8,128)(2,1)S(1)}, bf16[32,8192]{1,0:T(8,128)(2,1)}, u32[]{:S(2)}) copy-start(bf16[32,8192]{1,0:T(8,128)(2,1)} %grad_hbm.1) | copy-start | bytes 1572868
  0.6 56.7 %copy-start.1 = (bf16[32,8192]{1,0:T(8,128)(2,1)S(1)}, bf16[32,8192]{1,0:T(8,128)(2,1)}, u32[]{:S(2)}) copy-start(bf16[32,8192]{1,0:T(8,128)(2,1)} %value_hbm.1) | copy-start | bytes 1572868
  0.7 56.7 %copy-start = (bf16[32,8192]{1,0:T(8,128)(2,1)S(1)}, bf16[32,8192]{1,0:T(8,128)(2,1)}, u32[]{:S(2)}) copy-start(bf16[32,8192]{1,0:T(8,128)(2,1)} %key_hbm.1) | copy-start | bytes 1572868
  57.3 2.6 %copy-start.3 = (f32[64,256]{1,0:T(8,128)S(1)}, f32[64,256]{1,0:T(8,128)}, u32[]{:S(2)}) copy-start(f32[64,256]{1,0:T(8,128)} %get-tuple-element.18) | copy-start | bytes 196612

commit v3 on v2

--- a/solution.py
+++ b/solution.py
@@ -235,8 +235,8 @@
 def exchange_kernel(
     nctx, nch, chunks,
     query_hbm, key_hbm, value_hbm, grad_hbm, taps_ref,
-    out_ref, filt_ref,
-    query_ref, key_ref, value_ref, grad_ref, staged, landed, back, taps, sums, toeplitz, xt, ut, yt, zt,
+    conv_ref, corr_ref, filt_ref, key_ref, value_ref, grad_ref,
+    query_ref, staged, landed, back, taps, sums, toeplitz, xt, ut, yt, zt,
     in_send, in_recv, out_send, out_recv, tap_send, tap_recv, sum_send, sum_recv, local_sem, load_sem,
 ):
     ctx = lax.axis_index("ctx")
@@ -253,12 +253,14 @@
     per_block = block // tokens
     chunk_groups = CHUNK_CH // GROUP_CH
 
-    def partner(n):
-        order = n // nctx
-        step = (order % 2) * (0 - (order + 1) // 2) + (1 - order % 2) * (order // 2)
-        other_ch = (ch + nch // 2 + step + nch) % nch
-        other_ctx = (ctx + n + 1) % nctx
-        return other_ctx, other_ch
+    partners = []
+    for order in range(nch):
+        step = -(order + 1) // 2 if order % 2 else order // 2
+        other_ch = lax.rem(ch + (nch // 2 + step) % nch, nch)
+        for turn in range(1, nctx + 1):
+            if (nch // 2 + step) % nch or turn < nctx:
+                other_ctx = lax.rem(ctx + turn, nctx)
+                partners.append((other_ctx, other_ch, other_ctx * nch + other_ch))
 
     def columns(owner_ctx, owner_ch, chunk):
         start = owner_ch * (nctx * chans) + owner_ctx * chans + chunk * CHUNK_CH
@@ -272,52 +274,33 @@
             grad_ref[:, cols].astype(jnp.float32) * query_ref[:, cols].astype(jnp.float32)
         ).astype(jnp.bfloat16)
 
-    def in_copy(chunk, n):
-        other_ctx, other_ch = partner(n)
-        return pltpu.make_async_remote_copy(
-            src_ref=staged.at[:, columns(other_ctx, other_ch, chunk)],
-            dst_ref=landed.at[chunk, me],
-            send_sem=in_send.at[chunk, n],
-            recv_sem=in_recv.at[chunk, me],
-            device_id=(other_ctx, other_ch),
-            device_id_type=MESH,
-        )
-
-    def in_arrival(chunk, n):
-        other_ctx, other_ch = partner(n)
-        other = other_ctx * nch + other_ch
-        return pltpu.make_async_remote_copy(
-            src_ref=staged.at[:, columns(other_ctx, other_ch, chunk)],
-            dst_ref=landed.at[chunk, other],
-            send_sem=in_send.at[chunk, n],
-            recv_sem=in_recv.at[chunk, other],
-            device_id=(other_ctx, other_ch),
-            device_id_type=MESH,
-        )
-
-    def out_copy(chunk, n):
-        other_ctx, other_ch = partner(n)
-        other = other_ctx * nch + other_ch
-        return pltpu.make_async_remote_copy(
-            src_ref=back.at[chunk, other],
-            dst_ref=out_ref.at[:, columns(ctx, ch, chunk)],
-            send_sem=out_send.at[chunk, n],
-            recv_sem=out_recv.at[chunk, me],
-            device_id=(other_ctx, other_ch),
-            device_id_type=MESH,
-        )
-
-    def out_arrival(chunk, n):
-        other_ctx, other_ch = partner(n)
-        other = other_ctx * nch + other_ch
-        return pltpu.make_async_remote_copy(
-            src_ref=back.at[chunk, other],
-            dst_ref=out_ref.at[:, columns(other_ctx, other_ch, chunk)],
-            send_sem=out_send.at[chunk, n],
-            recv_sem=out_recv.at[chunk, other],
-            device_id=(other_ctx, other_ch),
-            device_id_type=MESH,
-        )
+    def send_in(chunk):
+        for other_ctx, other_ch, other in partners:
+            pltpu.make_async_remote_copy(
+                src_ref=staged.at[:, columns(other_ctx, other_ch, chunk)],
+                dst_ref=landed.at[chunk, me],
+                send_sem=in_send.at[chunk],
+                recv_sem=in_recv.at[chunk],
+                device_id=(other_ctx, other_ch),
+                device_id_type=MESH,
+            ).start()
+
+    def send_out(chunk):
+        own = columns(ctx, ch, chunk)
+        for other_ctx, other_ch, other in partners:
+            for half, dst in ((0, conv_ref), (tokens, corr_ref)):
+                pltpu.make_async_remote_copy(
+                    src_ref=back.at[chunk, other, pl.ds(half, tokens)],
+                    dst_ref=dst.at[:, own],
+                    send_sem=out_send.at[chunk],
+                    recv_sem=out_recv.at[chunk],
+                    device_id=(other_ctx, other_ch),
+                    device_id_type=MESH,
+                ).start()
+
+    def all_of(sem, chunk):
+        whole = landed.at[chunk, pl.ds(0, ndev - 1)]
+        pltpu.make_async_copy(whole, whole, sem.at[chunk]).wait()
 
     def tap_copy(step, sender):
         other = (ctx + step) % nctx
@@ -348,9 +331,12 @@
             staged.at[:, columns(ctx, ch, chunk)], landed.at[chunk, me], local_sem.at[chunk]
         )
 
-    def own_out(chunk):
+    def own_out(chunk, half):
+        dst = (conv_ref, corr_ref)[half]
         return pltpu.make_async_copy(
-            back.at[chunk, me], out_ref.at[:, columns(ctx, ch, chunk)], local_sem.at[chunks + chunk]
+            back.at[chunk, me, pl.ds(half * tokens, tokens)],
+            dst.at[:, columns(ctx, ch, chunk)],
+            local_sem.at[chunks + 2 * chunk + half],
         )
 
     def each(count, body, unroll=1):
@@ -379,11 +365,8 @@
 
     barrier = pltpu.get_barrier_semaphore()
 
-    def greet(n):
-        other_ctx, other_ch = partner(n)
+    for other_ctx, other_ch, _ in partners:
         pl.semaphore_signal(barrier, inc=1, device_id=(other_ctx, other_ch), device_id_type=MESH)
-
-    each(ndev - 1, greet)
 
     def gate_chunk(chunk, first, count):
         each(
@@ -397,7 +380,7 @@
     own_taps = pltpu.make_async_copy(
         taps_ref.at[pl.ds(pl.multiple_of(ctx * groups, 8), groups), :],
         taps.at[:, pl.ds(pl.multiple_of(ctx * span, 128), span)],
-        local_sem.at[2 * chunks],
+        local_sem.at[3 * chunks],
     )
     own_taps.start()
     for part in range(pieces):
@@ -407,11 +390,11 @@
     pl.semaphore_wait(barrier, ndev - 1)
     for step in range(1, nctx):
         tap_copy(step, True).start()
-    each(ndev - 1, lambda n: in_copy(0, n).start())
+    send_in(0)
     own_in(0).start()
     for chunk in range(1, chunks):
         gate_chunk(chunk, 0, ndev)
-        each(ndev - 1, lambda n: in_copy(chunk, n).start())
+        send_in(chunk)
         own_in(chunk).start()
     own_taps.wait()
     for step in range(1, nctx):
@@ -494,12 +477,13 @@
     each(groups, build, unroll=2)
     for chunk in range(chunks):
         own_in(chunk).wait()
-        each(ndev - 1, lambda n: in_arrival(chunk, n).wait_recv())
+        all_of(in_recv, chunk)
         turn_in(chunk)
         each(chunk_groups, lambda g: convolve(chunk, g), unroll=2)
         turn_out(chunk)
-        each(ndev - 1, lambda n: out_copy(chunk, n).start())
-        own_out(chunk).start()
+        send_out(chunk)
+        own_out(chunk, 0).start()
+        own_out(chunk, 1).start()
 
     for chunk in range(chunks):
         each(chunk_groups, lambda g: correlate(chunk, g), unroll=2)
@@ -509,17 +493,18 @@
     own_sums = pltpu.make_async_copy(
         sums.at[:, pl.ds(pl.multiple_of(ctx * span, 128), span)],
         filt_ref.at[pl.ds(pl.multiple_of(ctx * groups, 8), groups), :],
-        local_sem.at[2 * chunks + 1],
+        local_sem.at[3 * chunks + 1],
     )
     own_sums.start()
 
     for step in range(1, nctx):
         tap_copy(step, True).wait_send()
     for chunk in range(chunks):
-        each(ndev - 1, lambda n: in_copy(chunk, n).wait_send())
-        each(ndev - 1, lambda n: out_copy(chunk, n).wait_send())
-        each(ndev - 1, lambda n: out_arrival(chunk, n).wait_recv())
-        own_out(chunk).wait()
+        all_of(in_send, chunk)
+        all_of(out_send, chunk)
+        all_of(out_recv, chunk)
+        own_out(chunk, 0).wait()
+        own_out(chunk, 1).wait()
     for step in range(1, nctx):
         sum_copy(step, True).wait_send()
         sum_copy(step, False).wait_recv()
@@ -538,16 +523,18 @@
     vmem = pl.BlockSpec(memory_space=pltpu.VMEM)
     half = jnp.bfloat16
     sem = pltpu.SemaphoreType.DMA
-    returned, grad_filters = pl.pallas_call(
+    convolved, correlated, grad_filters, key_near, value_near, grad_near = pl.pallas_call(
         functools.partial(exchange_kernel, nctx, nch, chunks),
         out_shape=(
-            jax.ShapeDtypeStruct((2 * tokens, model), half),
+            jax.ShapeDtypeStruct((tokens, model), half),
+            jax.ShapeDtypeStruct((tokens, model), half),
             jax.ShapeDtypeStruct(long_filters.shape, jnp.float32),
-        ),
+        )
+        + (jax.ShapeDtypeStruct((tokens, model), half),) * 3,
         in_specs=[pl.BlockSpec(memory_space=pltpu.HBM)] * 4 + [vmem],
-        out_specs=(vmem, vmem),
-        scratch_shapes=[pltpu.VMEM((tokens, model), half)] * 4
-        + [
+        out_specs=(vmem,) * 6,
+        scratch_shapes=[
+            pltpu.VMEM((tokens, model), half),
             pltpu.VMEM((2 * tokens, model), half),
             pltpu.VMEM((chunks, ndev, 2 * tokens, CHUNK_CH), half),
             pltpu.VMEM((chunks, ndev, 2 * tokens, CHUNK_CH), half),
@@ -558,28 +545,28 @@
             pltpu.VMEM((chunks, chunk_groups, nblocks, GROUP_CH, TAPS_BLOCK), half),
             pltpu.VMEM((nblocks, CHUNK_CH, TAPS_BLOCK), half),
             pltpu.VMEM((nblocks, CHUNK_CH, TAPS_BLOCK), half),
-            sem((chunks, ndev)),
-            sem((chunks, ndev)),
-            sem((chunks, ndev)),
-            sem((chunks, ndev)),
+            sem((chunks,)),
+            sem((chunks,)),
+            sem((chunks,)),
+            sem((chunks,)),
             sem((nctx,)),
             sem((nctx,)),
             sem((nctx,)),
             sem((nctx,)),
-            sem((2 * chunks + 2,)),
+            sem((3 * chunks + 2,)),
             sem((4, LOAD_PIECES)),
         ],
         compiler_params=pltpu.CompilerParams(
-            collective_id=0, has_side_effects=True, vmem_limit_bytes=56 * 1024 * 1024
+            collective_id=0, has_side_effects=True, vmem_limit_bytes=51 * 1024 * 1024
         ),
         name="exchange_and_convolve",
     )(query_gate, key_gate, value_proj, grad_out, long_filters)
-    convolved = returned[:tokens].astype(jnp.float32)
-    correlated = returned[tokens:].astype(jnp.float32)
+    convolved = convolved.astype(jnp.float32)
+    correlated = correlated.astype(jnp.float32)
     return (
-        (grad_out.astype(jnp.float32) * convolved).astype(half),
-        (correlated * value_proj.astype(jnp.float32)).astype(half),
-        (correlated * key_gate.astype(jnp.float32)).astype(half),
+        (grad_near.astype(jnp.float32) * convolved).astype(half),
+        (correlated * value_near.astype(jnp.float32)).astype(half),
+        (correlated * key_near.astype(jnp.float32)).astype(half),
         grad_filters,
     )
 

time: 60.7 us -> 55.6 us (0.916)
  Pallas kernels: 56.6 us -> 52 us
  other arithmetic: 2.58 us -> 1.35 us
  local copies, waits for them, and re-layouts: 0.65 us -> 1.46 us
    pallas_call x1, Pallas kernels: 56.6 us -> 52 us  [one_exchange(): pl.pallas_call(functools.partial(exchange_kernel, nctx, nch, chunks), out...]
    convert_element_type x1, other arithmetic: 2.58 us -> 1.35 us  [one_exchange(): (correlated * key_near.astype(jnp.float32)).astype(half)]
    unnamed x9 -> x3, local copies, waits for them, and re-layouts: 0.65 us -> 1.46 us
where the time goes in v3:
time: 55.6 us; the launch traced here: 55.4 us
  Pallas kernels  52 us (94%)
  local copies, waits for them, and re-layouts  1.46 us (3%)
  other arithmetic  1.35 us (2%)
  between operations  0.65 us (1%)
    pallas_call x1, Pallas kernels, one_exchange(): pl.pallas_call(functools.partial(exchange_kernel, nctx, nch, chunks), out...  52 us
    unnamed x3, local copies, waits for them, and re-layouts  1.46 us
    convert_element_type x1, other arithmetic, one_exchange(): (correlated * key_near.astype(jnp.float32)).astype(half)  1.35 us

profile of v3, /device:TPU:0, one launch (start us, length us, event | category | flops | bytes accessed | tf_op | source)
XLA Modules:
  0.0 55.4 jit_solution(7037577457492634332)
XLA Ops:
  0.6 0.0 copy-start
  0.6 0.8 %copy-done = f32[64,256]{1,0:T(8,128)S(1)} copy-done((f32[64,256]{1,0:T(8,128)S(1)}, f32[64,256]{1,0:T(8,128)}, u32[]{:S(2)}) %copy-start) | copy-done | bytes 65560
  1.5 52.0 %exchange_and_convolve.1 = (bf16[32,8192]{1,0:T(8,128)(2,1)S(1)}, bf16[32,8192]{1,0:T(8,128)(2,1)S(1)}, f32[64,256]{1,0:T(8,128)S(1)}, bf16[32,8192]{1,0:T(8,128...) custom-call(bf16[32,8192]{1,0:T(8,128)(2,1)} %query_hbm.1, bf16[32,8192]{1,0:T(8,128)(2,1)} %key_hbm.1, ...), custom_call_target="tpu_custom_call" | custom-call | tf_op jit(solution)/shard_map/exchange_and_convolve/pallas_call | solution.py:526
  53.4 1.4 %fusion.1 = (bf16[32,8192]{1,0:T(8,128)(2,1)}, bf16[32,8192]{1,0:T(8,128)(2,1)}, bf16[32,8192]{1,0:T(8,128)(2,1)}) fusion(bf16[32,8192]{1,0:T(8,128)(2,1)S(1)} %get-tuple-element.12, bf16[32,8192]{1,0:T(8,128)(2,1)S(1)} %get-tuple-element.14, bf16[32,8192]{1,0:T(8,128)(2,1)S(1)} %get-tuple-element.13, bf16[32,8192]{1,0:T(8,128)(2,1)S(1)} %get-tuple-element.11, ...), kind=kLoop, calls=%fused_computation.3 | loop fusion | flops 2883584 | bytes 4194304 | tf_op jit(solution)/shard_map/convert_element_type | solution.py:569
  54.8 0.6 %copy.10 = f32[64,256]{1,0:T(8,128)} copy(f32[64,256]{1,0:T(8,128)S(1)} %get-tuple-element.26) | data formatting | bytes 131072
Async XLA Ops:
  0.6 0.8 %copy-start = (f32[64,256]{1,0:T(8,128)S(1)}, f32[64,256]{1,0:T(8,128)}, u32[]{:S(2)}) copy-start(f32[64,256]{1,0:T(8,128)} %taps_ref.1) | copy-start | bytes 196612

commit v4 on v3

--- a/solution.py
+++ b/solution.py
@@ -227,7 +227,6 @@
 
 TAPS_BLOCK = 128
 CHUNK_CH = 128
-LOAD_PIECES = 4
 MESH = pl.DeviceIdType.MESH
 NT = (((1,), (1,)), ((), ()))
 
@@ -236,7 +235,7 @@
     nctx, nch, chunks,
     query_hbm, key_hbm, value_hbm, grad_hbm, taps_ref,
     conv_ref, corr_ref, filt_ref, key_ref, value_ref, grad_ref,
-    query_ref, staged, landed, back, taps, sums, toeplitz, xt, ut, yt, zt,
+    query_ref, staged, landed, back, taps, sums, toeplitz, turned, result,
     in_send, in_recv, out_send, out_recv, tap_send, tap_recv, sum_send, sum_recv, local_sem, load_sem,
 ):
     ctx = lax.axis_index("ctx")
@@ -252,55 +251,61 @@
     nblocks = seq // block
     per_block = block // tokens
     chunk_groups = CHUNK_CH // GROUP_CH
-
-    partners = []
+    phases = 2 * chunks
+
+    rounds = []
     for order in range(nch):
         step = -(order + 1) // 2 if order % 2 else order // 2
-        other_ch = lax.rem(ch + (nch // 2 + step) % nch, nch)
+        offset = (nch // 2 + step) % nch
+        other_ch = lax.rem(ch + offset, nch)
+        turns = []
         for turn in range(1, nctx + 1):
-            if (nch // 2 + step) % nch or turn < nctx:
+            if offset or turn < nctx:
                 other_ctx = lax.rem(ctx + turn, nctx)
-                partners.append((other_ctx, other_ch, other_ctx * nch + other_ch))
+                turns.append((other_ctx, other_ctx * nch + other_ch))
+        rounds.append((other_ch, turns))
 
     def columns(owner_ctx, owner_ch, chunk):
         start = owner_ch * (nctx * chans) + owner_ctx * chans + chunk * CHUNK_CH
         return pl.ds(pl.multiple_of(start, 128), CHUNK_CH)
 
-    def gate(cols):
-        staged[0:tokens, cols] = (
-            key_ref[:, cols].astype(jnp.float32) * value_ref[:, cols].astype(jnp.float32)
-        ).astype(jnp.bfloat16)
-        staged[tokens:, cols] = (
-            grad_ref[:, cols].astype(jnp.float32) * query_ref[:, cols].astype(jnp.float32)
-        ).astype(jnp.bfloat16)
-
-    def send_in(chunk):
-        for other_ctx, other_ch, other in partners:
+    def gate(phase, other_ch):
+        near, far = ((key_ref, value_ref), (grad_ref, query_ref))[phase % 2]
+        rows = pl.ds(phase % 2 * tokens, tokens)
+        for owner in range(nctx):
+            cols = columns(owner, other_ch, phase // 2)
+            staged[rows, cols] = (
+                near[:, cols].astype(jnp.float32) * far[:, cols].astype(jnp.float32)
+            ).astype(jnp.bfloat16)
+
+    def send_in(phase, other_ch, turns):
+        rows = pl.ds(phase % 2 * tokens, tokens)
+        for other_ctx, _ in turns:
             pltpu.make_async_remote_copy(
-                src_ref=staged.at[:, columns(other_ctx, other_ch, chunk)],
-                dst_ref=landed.at[chunk, me],
-                send_sem=in_send.at[chunk],
-                recv_sem=in_recv.at[chunk],
+                src_ref=staged.at[rows, columns(other_ctx, other_ch, phase // 2)],
+                dst_ref=landed.at[phase, me],
+                send_sem=in_send.at[phase],
+                recv_sem=in_recv.at[phase],
                 device_id=(other_ctx, other_ch),
                 device_id_type=MESH,
             ).start()
 
-    def send_out(chunk):
-        own = columns(ctx, ch, chunk)
-        for other_ctx, other_ch, other in partners:
-            for half, dst in ((0, conv_ref), (tokens, corr_ref)):
+    def send_out(phase):
+        own = columns(ctx, ch, phase // 2)
+        for other_ch, turns in rounds:
+            for other_ctx, other in turns:
                 pltpu.make_async_remote_copy(
-                    src_ref=back.at[chunk, other, pl.ds(half, tokens)],
-                    dst_ref=dst.at[:, own],
-                    send_sem=out_send.at[chunk],
-                    recv_sem=out_recv.at[chunk],
+                    src_ref=back.at[phase, other],
+                    dst_ref=(conv_ref, corr_ref)[phase % 2].at[:, own],
+                    send_sem=out_send.at[phase],
+                    recv_sem=out_recv.at[phase],
                     device_id=(other_ctx, other_ch),
                     device_id_type=MESH,
                 ).start()
 
-    def all_of(sem, chunk):
-        whole = landed.at[chunk, pl.ds(0, ndev - 1)]
-        pltpu.make_async_copy(whole, whole, sem.at[chunk]).wait()
+    def all_of(sem, phase):
+        whole = landed.at[phase, pl.ds(0, ndev - 1)]
+        pltpu.make_async_copy(whole, whole, sem.at[phase]).wait()
 
     def tap_copy(step, sender):
         other = (ctx + step) % nctx
@@ -326,17 +331,18 @@
             device_id_type=MESH,
         )
 
-    def own_in(chunk):
+    def own_in(phase):
         return pltpu.make_async_copy(
-            staged.at[:, columns(ctx, ch, chunk)], landed.at[chunk, me], local_sem.at[chunk]
-        )
-
-    def own_out(chunk, half):
-        dst = (conv_ref, corr_ref)[half]
+            staged.at[pl.ds(phase % 2 * tokens, tokens), columns(ctx, ch, phase // 2)],
+            landed.at[phase, me],
+            local_sem.at[phase],
+        )
+
+    def own_out(phase):
         return pltpu.make_async_copy(
-            back.at[chunk, me, pl.ds(half * tokens, tokens)],
-            dst.at[:, columns(ctx, ch, chunk)],
-            local_sem.at[chunks + 2 * chunk + half],
+            back.at[phase, me],
+            (conv_ref, corr_ref)[phase % 2].at[:, columns(ctx, ch, phase // 2)],
+            local_sem.at[phases + phase],
         )
 
     def each(count, body, unroll=1):
@@ -346,56 +352,45 @@
 
         lax.fori_loop(0, count, step, 0, unroll=unroll)
 
-    pieces = LOAD_PIECES
-    piece = nctx * nch * chans // pieces
-
-    def load(which, part):
+    def load(which, order):
         src, dst = (
-            (query_hbm, query_ref),
             (key_hbm, key_ref),
             (value_hbm, value_ref),
             (grad_hbm, grad_ref),
+            (query_hbm, query_ref),
         )[which]
-        cols = pl.ds(part * piece, piece)
-        return pltpu.make_async_copy(src.at[:, cols], dst.at[:, cols], load_sem.at[which, part])
-
-    for part in range(pieces):
-        for which in range(4):
-            load(which, part).start()
+        piece = nctx * chans
+        cols = pl.ds(pl.multiple_of(rounds[order][0] * piece, 128), piece)
+        return pltpu.make_async_copy(src.at[:, cols], dst.at[:, cols], load_sem.at[which, order])
 
     barrier = pltpu.get_barrier_semaphore()
-
-    for other_ctx, other_ch, _ in partners:
-        pl.semaphore_signal(barrier, inc=1, device_id=(other_ctx, other_ch), device_id_type=MESH)
-
-    def gate_chunk(chunk, first, count):
-        each(
-            count,
-            lambda n: gate(
-                pl.ds(pl.multiple_of((first + n) * chans + chunk * CHUNK_CH, 128), CHUNK_CH)
-            ),
-            unroll=4,
-        )
-
+    for other_ch, turns in rounds:
+        for other_ctx, _ in turns:
+            pl.semaphore_signal(
+                barrier, inc=1, device_id=(other_ctx, other_ch), device_id_type=MESH
+            )
+    for kind in range(2):
+        for order in range(nch):
+            load(2 * kind, order).start()
+            load(2 * kind + 1, order).start()
     own_taps = pltpu.make_async_copy(
         taps_ref.at[pl.ds(pl.multiple_of(ctx * groups, 8), groups), :],
         taps.at[:, pl.ds(pl.multiple_of(ctx * span, 128), span)],
-        local_sem.at[3 * chunks],
+        local_sem.at[2 * phases],
     )
     own_taps.start()
-    for part in range(pieces):
-        for which in range(4):
-            load(which, part).wait()
-        gate_chunk(0, part * (ndev // pieces), ndev // pieces)
-    pl.semaphore_wait(barrier, ndev - 1)
-    for step in range(1, nctx):
-        tap_copy(step, True).start()
-    send_in(0)
-    own_in(0).start()
-    for chunk in range(1, chunks):
-        gate_chunk(chunk, 0, ndev)
-        send_in(chunk)
-        own_in(chunk).start()
+    for phase in range(phases):
+        for order, (other_ch, turns) in enumerate(rounds):
+            if phase < 2:
+                load(2 * phase, order).wait()
+                load(2 * phase + 1, order).wait()
+            gate(phase, other_ch)
+            if phase == 0 and order == 0:
+                pl.semaphore_wait(barrier, ndev - 1)
+                for step in range(1, nctx):
+                    tap_copy(step, True).start()
+            send_in(phase, other_ch, turns)
+        own_in(phase).start()
     own_taps.wait()
     for step in range(1, nctx):
         tap_copy(step, False).wait_recv()
@@ -415,19 +410,10 @@
             [padded[k * GROUP_CH : k * GROUP_CH + block] for k in range(nblocks)], axis=1
         )
 
-    def earlier(stack):
-        padded = jnp.concatenate([zeros, stack], axis=0)
-        return jnp.concatenate(
-            [padded[block - k * GROUP_CH : 2 * block - k * GROUP_CH] for k in range(nblocks)],
-            axis=1,
-        )
-
-    def turn_in(chunk):
+    def turn_in(phase):
         for i in range(nblocks):
-            src = pl.ds(i * per_block, per_block)
-            for rows, dst in ((pl.ds(0, tokens), xt), (pl.ds(tokens, tokens), ut)):
-                tile = landed[chunk, src, rows, :].reshape(block, CHUNK_CH)
-                dst[chunk, :, i] = tile.T.reshape(chunk_groups, GROUP_CH, block)
+            tile = landed[phase, pl.ds(i * per_block, per_block)].reshape(block, CHUNK_CH)
+            turned[phase, :, i] = tile.T.reshape(chunk_groups, GROUP_CH, block)
 
     def build(group):
         row = taps[pl.ds(group, 1), :]
@@ -439,51 +425,67 @@
             for k in range(nblocks):
                 toeplitz[group, which, k] = part[:, k * block : (k + 1) * block]
 
-    def convolve(chunk, g):
-        x_cat = earlier(xt[chunk, g].reshape(block, block))
-        u_cat = later(ut[chunk, g].reshape(block, block))
-        conv = jnp.zeros((block, block), jnp.float32)
-        corr = jnp.zeros((block, block), jnp.float32)
-        for which in range(2):
-            part = toeplitz[chunk * chunk_groups + g, which]
-            tall = part.reshape(nblocks * block, block)
-            flat = jnp.concatenate([part[k] for k in range(nblocks)], axis=1)
-            conv = conv + jnp.dot(x_cat, tall, preferred_element_type=jnp.float32)
-            corr = corr + lax.dot_general(u_cat, flat, NT, preferred_element_type=jnp.float32)
-        yt[:, pl.ds(pl.multiple_of(g * GROUP_CH, GROUP_CH), GROUP_CH), :] = (
-            conv.astype(jnp.bfloat16).reshape(nblocks, GROUP_CH, block)
-        )
-        zt[:, pl.ds(pl.multiple_of(g * GROUP_CH, GROUP_CH), GROUP_CH), :] = (
-            corr.astype(jnp.bfloat16).reshape(nblocks, GROUP_CH, block)
-        )
-
-    def turn_out(chunk):
+    def convolve(phase, g):
+        stack = turned[phase, g].reshape(block, block)
+        edge = jnp.zeros((GROUP_CH, block), jnp.bfloat16)
+        group = phase // 2 * chunk_groups + g
+        total = None
+        for pair in range(nblocks // 2):
+            cut = 2 * pair * GROUP_CH
+            high, low = [
+                [toeplitz[group, which, 2 * pair + k] for k in range(2)] for which in range(2)
+            ]
+            if phase % 2 == 0:
+                shifted = jnp.concatenate([edge, stack[: block - cut - GROUP_CH]], axis=0)
+                left = jnp.concatenate([stack[: block - cut], shifted], axis=1)
+                right = jnp.concatenate(
+                    [jnp.concatenate(high, axis=0), jnp.concatenate(low, axis=0)], axis=1
+                )
+                both = jnp.dot(left, right, preferred_element_type=jnp.float32)
+            else:
+                shifted = jnp.concatenate([stack[cut + GROUP_CH :], edge], axis=0)
+                left = jnp.concatenate([stack[cut:], shifted], axis=1)
+                right = jnp.concatenate(
+                    [jnp.concatenate(high, axis=1), jnp.concatenate(low, axis=1)], axis=0
+                )
+                both = lax.dot_general(left, right, NT, preferred_element_type=jnp.float32)
+            part = both[:, :block] + both[:, block:]
+            if pair:
+                blank = jnp.zeros((cut, block), jnp.float32)
+                part = jnp.concatenate([blank, part] if phase % 2 == 0 else [part, blank], axis=0)
+                total = total + part
+            else:
+                total = part
+        result[phase % 2, :, pl.ds(pl.multiple_of(g * GROUP_CH, GROUP_CH), GROUP_CH), :] = (
+            total.astype(jnp.bfloat16).reshape(nblocks, GROUP_CH, block)
+        )
+
+    def turn_out(phase):
         for i in range(nblocks):
-            dst = pl.ds(i * per_block, per_block)
-            back[chunk, dst, 0:tokens, :] = yt[i].T.reshape(per_block, tokens, CHUNK_CH)
-            back[chunk, dst, tokens:, :] = zt[i].T.reshape(per_block, tokens, CHUNK_CH)
+            back[phase, pl.ds(i * per_block, per_block)] = result[phase % 2, i].T.reshape(
+                per_block, tokens, CHUNK_CH
+            )
 
     def correlate(chunk, g):
-        stack_x = xt[chunk, g].reshape(block, block)
-        u_cat = later(ut[chunk, g].reshape(block, block))
-        turned = lax.dot_general(
+        stack_x = turned[2 * chunk, g].reshape(block, block)
+        u_cat = later(turned[2 * chunk + 1, g].reshape(block, block))
+        mirrored = lax.dot_general(
             flip, stack_x, NT, preferred_element_type=jnp.float32
         ).astype(jnp.bfloat16)
-        pairs = jnp.dot(turned, u_cat, preferred_element_type=jnp.float32)
+        pairs = jnp.dot(mirrored, u_cat, preferred_element_type=jnp.float32)
         pairs = jnp.concatenate([pairs, jnp.zeros((block, block), jnp.float32)], axis=1)
         total = jnp.sum(slide(pairs, 1), axis=0, keepdims=True)
         sums[pl.ds(chunk * chunk_groups + g, 1), :] = total
 
     each(groups, build, unroll=2)
-    for chunk in range(chunks):
-        own_in(chunk).wait()
-        all_of(in_recv, chunk)
-        turn_in(chunk)
-        each(chunk_groups, lambda g: convolve(chunk, g), unroll=2)
-        turn_out(chunk)
-        send_out(chunk)
-        own_out(chunk, 0).start()
-        own_out(chunk, 1).start()
+    for phase in range(phases):
+        own_in(phase).wait()
+        all_of(in_recv, phase)
+        turn_in(phase)
+        each(chunk_groups, lambda g: convolve(phase, g), unroll=2)
+        turn_out(phase)
+        send_out(phase)
+        own_out(phase).start()
 
     for chunk in range(chunks):
         each(chunk_groups, lambda g: correlate(chunk, g), unroll=2)
@@ -493,18 +495,17 @@
     own_sums = pltpu.make_async_copy(
         sums.at[:, pl.ds(pl.multiple_of(ctx * span, 128), span)],
         filt_ref.at[pl.ds(pl.multiple_of(ctx * groups, 8), groups), :],
-        local_sem.at[3 * chunks + 1],
+        local_sem.at[2 * phases + 1],
     )
     own_sums.start()
 
     for step in range(1, nctx):
         tap_copy(step, True).wait_send()
-    for chunk in range(chunks):
-        all_of(in_send, chunk)
-        all_of(out_send, chunk)
-        all_of(out_recv, chunk)
-        own_out(chunk, 0).wait()
-        own_out(chunk, 1).wait()
+    for phase in range(phases):
+        all_of(in_send, phase)
+        all_of(out_send, phase)
+        all_of(out_recv, phase)
+        own_out(phase).wait()
     for step in range(1, nctx):
         sum_copy(step, True).wait_send()
         sum_copy(step, False).wait_recv()
@@ -531,30 +532,28 @@
             jax.ShapeDtypeStruct(long_filters.shape, jnp.float32),
         )
         + (jax.ShapeDtypeStruct((tokens, model), half),) * 3,
-        in_specs=[pl.BlockSpec(memory_space=pltpu.HBM)] * 4 + [vmem],
+        in_specs=[pl.BlockSpec(memory_space=pltpu.HBM)] * 5,
         out_specs=(vmem,) * 6,
         scratch_shapes=[
             pltpu.VMEM((tokens, model), half),
             pltpu.VMEM((2 * tokens, model), half),
-            pltpu.VMEM((chunks, ndev, 2 * tokens, CHUNK_CH), half),
-            pltpu.VMEM((chunks, ndev, 2 * tokens, CHUNK_CH), half),
+            pltpu.VMEM((2 * chunks, ndev, tokens, CHUNK_CH), half),
+            pltpu.VMEM((2 * chunks, ndev, tokens, CHUNK_CH), half),
             pltpu.VMEM((groups, seq), jnp.float32),
             pltpu.VMEM((groups, seq), jnp.float32),
             pltpu.VMEM((groups, 2, nblocks, TAPS_BLOCK, TAPS_BLOCK), half),
-            pltpu.VMEM((chunks, chunk_groups, nblocks, GROUP_CH, TAPS_BLOCK), half),
-            pltpu.VMEM((chunks, chunk_groups, nblocks, GROUP_CH, TAPS_BLOCK), half),
-            pltpu.VMEM((nblocks, CHUNK_CH, TAPS_BLOCK), half),
-            pltpu.VMEM((nblocks, CHUNK_CH, TAPS_BLOCK), half),
-            sem((chunks,)),
-            sem((chunks,)),
-            sem((chunks,)),
-            sem((chunks,)),
+            pltpu.VMEM((2 * chunks, chunk_groups, nblocks, GROUP_CH, TAPS_BLOCK), half),
+            pltpu.VMEM((2, nblocks, CHUNK_CH, TAPS_BLOCK), half),
+            sem((2 * chunks,)),
+            sem((2 * chunks,)),
+            sem((2 * chunks,)),
+            sem((2 * chunks,)),
             sem((nctx,)),
             sem((nctx,)),
             sem((nctx,)),
             sem((nctx,)),
-            sem((3 * chunks + 2,)),
-            sem((4, LOAD_PIECES)),
+            sem((4 * chunks + 2,)),
+            sem((4, nch)),
         ],
         compiler_params=pltpu.CompilerParams(
             collective_id=0, has_side_effects=True, vmem_limit_bytes=51 * 1024 * 1024

time: 55.6 us -> 56.7 us (1.020)
  Pallas kernels: 52 us -> 53 us
    pallas_call x1, Pallas kernels: 52 us -> 53 us  [one_exchange(): pl.pallas_call(functools.partial(exchange_kernel, nctx, nch, chunks), out...]
where the time goes in v4:
time: 56.7 us; the launch traced here: 56.5 us
  Pallas kernels  53 us (93%)
  local copies, waits for them, and re-layouts  1.46 us (3%)
  other arithmetic  1.35 us (2%)
  between operations  0.65 us (1%)
    pallas_call x1, Pallas kernels, one_exchange(): pl.pallas_call(functools.partial(exchange_kernel, nctx, nch, chunks), out...  53 us
    unnamed x3, local copies, waits for them, and re-layouts  1.46 us
    convert_element_type x1, other arithmetic, one_exchange(): (correlated * key_near.astype(jnp.float32)).astype(half)  1.35 us

profile of v4, /device:TPU:0, one launch (start us, length us, event | category | flops | bytes accessed | tf_op | source)
XLA Modules:
  0.0 56.5 jit_solution(2506863659598011560)
XLA Ops:
  0.6 0.0 copy-start
  0.6 0.8 %copy-done = f32[64,256]{1,0:T(8,128)S(1)} copy-done((f32[64,256]{1,0:T(8,128)S(1)}, f32[64,256]{1,0:T(8,128)}, u32[]{:S(2)}) %copy-start) | copy-done | bytes 65560
  1.5 53.0 %exchange_and_convolve.1 = (bf16[32,8192]{1,0:T(8,128)(2,1)S(1)}, bf16[32,8192]{1,0:T(8,128)(2,1)S(1)}, f32[64,256]{1,0:T(8,128)S(1)}, bf16[32,8192]{1,0:T(8,128...) custom-call(bf16[32,8192]{1,0:T(8,128)(2,1)} %query_hbm.1, bf16[32,8192]{1,0:T(8,128)(2,1)} %key_hbm.1, ...), custom_call_target="tpu_custom_call" | custom-call | tf_op jit(solution)/shard_map/exchange_and_convolve/pallas_call | solution.py:527
  54.5 1.4 %fusion.1 = (bf16[32,8192]{1,0:T(8,128)(2,1)}, bf16[32,8192]{1,0:T(8,128)(2,1)}, bf16[32,8192]{1,0:T(8,128)(2,1)}) fusion(bf16[32,8192]{1,0:T(8,128)(2,1)S(1)} %get-tuple-element.12, bf16[32,8192]{1,0:T(8,128)(2,1)S(1)} %get-tuple-element.14, bf16[32,8192]{1,0:T(8,128)(2,1)S(1)} %get-tuple-element.13, bf16[32,8192]{1,0:T(8,128)(2,1)S(1)} %get-tuple-element.11, ...), kind=kLoop, calls=%fused_computation.3 | loop fusion | flops 2883584 | bytes 4194304 | tf_op jit(solution)/shard_map/convert_element_type | solution.py:568
  55.9 0.6 %copy.10 = f32[64,256]{1,0:T(8,128)} copy(f32[64,256]{1,0:T(8,128)S(1)} %get-tuple-element.26) | data formatting | bytes 131072
Async XLA Ops:
  0.6 0.8 %copy-start = (f32[64,256]{1,0:T(8,128)S(1)}, f32[64,256]{1,0:T(8,128)}, u32[]{:S(2)}) copy-start(f32[64,256]{1,0:T(8,128)} %taps_ref.1) | copy-start | bytes 196612

commit v5 on v3

--- a/solution.py
+++ b/solution.py
@@ -253,14 +253,18 @@
     per_block = block // tokens
     chunk_groups = CHUNK_CH // GROUP_CH
 
+    offsets = []
+    for order in range(nch // 2):
+        far = nch // 2 + (-(order + 1) // 2 if order % 2 else order // 2)
+        offsets.append((far, (far + nch // 2) % nch))
     partners = []
-    for order in range(nch):
-        step = -(order + 1) // 2 if order % 2 else order // 2
-        other_ch = lax.rem(ch + (nch // 2 + step) % nch, nch)
+    for pair in offsets:
         for turn in range(1, nctx + 1):
-            if (nch // 2 + step) % nch or turn < nctx:
-                other_ctx = lax.rem(ctx + turn, nctx)
-                partners.append((other_ctx, other_ch, other_ctx * nch + other_ch))
+            for offset in pair:
+                if offset or turn < nctx:
+                    other_ch = lax.rem(ch + offset, nch)
+                    other_ctx = lax.rem(ctx + turn, nctx)
+                    partners.append((other_ctx, other_ch, other_ctx * nch + other_ch))
 
     def columns(owner_ctx, owner_ch, chunk):
         start = owner_ch * (nctx * chans) + owner_ctx * chans + chunk * CHUNK_CH

time: 55.6 us -> 55.4 us (level)
  no operation moved by 1% of the time
where the time goes in v5:
time: 55.4 us; the launch traced here: 55 us
  Pallas kernels  51.6 us (93%)
  local copies, waits for them, and re-layouts  1.46 us (3%)
  other arithmetic  1.35 us (2%)
  between operations  0.65 us (1%)
    pallas_call x1, Pallas kernels, one_exchange(): pl.pallas_call(functools.partial(exchange_kernel, nctx, nch, chunks), out...  51.6 us
    unnamed x3, local copies, waits for them, and re-layouts  1.46 us
    convert_element_type x1, other arithmetic, one_exchange(): (correlated * key_near.astype(jnp.float32)).astype(half)  1.35 us

profile of v5, /device:TPU:0, one launch (start us, length us, event | category | flops | bytes accessed | tf_op | source)
XLA Modules:
  0.0 55.0 jit_solution(1281602348281233191)
XLA Ops:
  0.6 0.0 copy-start
  0.6 0.8 %copy-done = f32[64,256]{1,0:T(8,128)S(1)} copy-done((f32[64,256]{1,0:T(8,128)S(1)}, f32[64,256]{1,0:T(8,128)}, u32[]{:S(2)}) %copy-start) | copy-done | bytes 65560
  1.5 51.6 %exchange_and_convolve.1 = (bf16[32,8192]{1,0:T(8,128)(2,1)S(1)}, bf16[32,8192]{1,0:T(8,128)(2,1)S(1)}, f32[64,256]{1,0:T(8,128)S(1)}, bf16[32,8192]{1,0:T(8,128...) custom-call(bf16[32,8192]{1,0:T(8,128)(2,1)} %query_hbm.1, bf16[32,8192]{1,0:T(8,128)(2,1)} %key_hbm.1, ...), custom_call_target="tpu_custom_call" | custom-call | tf_op jit(solution)/shard_map/exchange_and_convolve/pallas_call | solution.py:530
  53.1 1.4 %fusion.1 = (bf16[32,8192]{1,0:T(8,128)(2,1)}, bf16[32,8192]{1,0:T(8,128)(2,1)}, bf16[32,8192]{1,0:T(8,128)(2,1)}) fusion(bf16[32,8192]{1,0:T(8,128)(2,1)S(1)} %get-tuple-element.12, bf16[32,8192]{1,0:T(8,128)(2,1)S(1)} %get-tuple-element.14, bf16[32,8192]{1,0:T(8,128)(2,1)S(1)} %get-tuple-element.13, bf16[32,8192]{1,0:T(8,128)(2,1)S(1)} %get-tuple-element.11, ...), kind=kLoop, calls=%fused_computation.3 | loop fusion | flops 2883584 | bytes 4194304 | tf_op jit(solution)/shard_map/convert_element_type | solution.py:573
  54.4 0.6 %copy.10 = f32[64,256]{1,0:T(8,128)} copy(f32[64,256]{1,0:T(8,128)S(1)} %get-tuple-element.26) | data formatting | bytes 131072
Async XLA Ops:
  0.6 0.8 %copy-start = (f32[64,256]{1,0:T(8,128)S(1)}, f32[64,256]{1,0:T(8,128)}, u32[]{:S(2)}) copy-start(f32[64,256]{1,0:T(8,128)} %taps_ref.1) | copy-start | bytes 196612

commit v6 on v5

--- a/solution.py
+++ b/solution.py
@@ -410,8 +410,19 @@
     zeros = jnp.zeros((block, block), jnp.bfloat16)
     width = block + seq
 
-    def slide(values, shift):
-        return pltpu.roll(values, shift, 1, stride=1, stride_axis=0)[:, block:]
+    doubling = [8 << n for n in range((block // 8).bit_length() - 1)]
+
+    def spread_diagonals(row):
+        wide = pltpu.roll(jnp.broadcast_to(row, (8, width)), 0, 1, stride=1, stride_axis=0)
+        for rows in doubling:
+            wide = jnp.concatenate([wide, pltpu.roll(wide, rows, 1)], axis=0)
+        return wide[:, block:]
+
+    def sum_diagonals(values):
+        for rows in doubling[::-1]:
+            values = values[:rows] + pltpu.roll(values[rows:], rows, 1)
+        values = pltpu.roll(values, 1, 1, stride=1, stride_axis=0)[:, block:]
+        return jnp.sum(values, axis=0, keepdims=True)
 
     def later(stack):
         padded = jnp.concatenate([stack, zeros], axis=0)
@@ -436,7 +447,7 @@
     def build(group):
         row = taps[pl.ds(group, 1), :]
         row = jnp.concatenate([jnp.zeros((1, block), jnp.float32), row], axis=1)
-        wide = slide(jnp.broadcast_to(row, (block, width)), 0)
+        wide = spread_diagonals(row)
         high = wide.astype(jnp.bfloat16)
         low = (wide - high.astype(jnp.float32)).astype(jnp.bfloat16)
         for which, part in ((0, high), (1, low)):
@@ -475,8 +486,7 @@
         ).astype(jnp.bfloat16)
         pairs = jnp.dot(turned, u_cat, preferred_element_type=jnp.float32)
         pairs = jnp.concatenate([pairs, jnp.zeros((block, block), jnp.float32)], axis=1)
-        total = jnp.sum(slide(pairs, 1), axis=0, keepdims=True)
-        sums[pl.ds(chunk * chunk_groups + g, 1), :] = total
+        sums[pl.ds(chunk * chunk_groups + g, 1), :] = sum_diagonals(pairs)
 
     each(groups, build, unroll=2)
     for chunk in range(chunks):

time: 55.4 us -> 55.4 us (level)
  no operation moved by 1% of the time
where the time goes in v6:
time: 55.4 us; the launch traced here: 55 us
  Pallas kernels  51.6 us (93%)
  local copies, waits for them, and re-layouts  1.46 us (3%)
  other arithmetic  1.35 us (2%)
  between operations  0.65 us (1%)
    pallas_call x1, Pallas kernels, one_exchange(): pl.pallas_call(functools.partial(exchange_kernel, nctx, nch, chunks), out...  51.6 us
    unnamed x3, local copies, waits for them, and re-layouts  1.46 us
    convert_element_type x1, other arithmetic, one_exchange(): (correlated * key_near.astype(jnp.float32)).astype(half)  1.35 us

profile of v6, /device:TPU:0, one launch (start us, length us, event | category | flops | bytes accessed | tf_op | source)
XLA Modules:
  0.0 55.0 jit_solution(502582891213080038)
XLA Ops:
  0.6 0.0 copy-start
  0.6 0.8 %copy-done = f32[64,256]{1,0:T(8,128)S(1)} copy-done((f32[64,256]{1,0:T(8,128)S(1)}, f32[64,256]{1,0:T(8,128)}, u32[]{:S(2)}) %copy-start) | copy-done | bytes 65560
  1.5 51.6 %exchange_and_convolve.1 = (bf16[32,8192]{1,0:T(8,128)(2,1)S(1)}, bf16[32,8192]{1,0:T(8,128)(2,1)S(1)}, f32[64,256]{1,0:T(8,128)S(1)}, bf16[32,8192]{1,0:T(8,128...) custom-call(bf16[32,8192]{1,0:T(8,128)(2,1)} %query_hbm.1, bf16[32,8192]{1,0:T(8,128)(2,1)} %key_hbm.1, ...), custom_call_target="tpu_custom_call" | custom-call | tf_op jit(solution)/shard_map/exchange_and_convolve/pallas_call | solution.py:540
  53.1 1.4 %fusion.1 = (bf16[32,8192]{1,0:T(8,128)(2,1)}, bf16[32,8192]{1,0:T(8,128)(2,1)}, bf16[32,8192]{1,0:T(8,128)(2,1)}) fusion(bf16[32,8192]{1,0:T(8,128)(2,1)S(1)} %get-tuple-element.12, bf16[32,8192]{1,0:T(8,128)(2,1)S(1)} %get-tuple-element.14, bf16[32,8192]{1,0:T(8,128)(2,1)S(1)} %get-tuple-element.13, bf16[32,8192]{1,0:T(8,128)(2,1)S(1)} %get-tuple-element.11, ...), kind=kLoop, calls=%fused_computation.3 | loop fusion | flops 2883584 | bytes 4194304 | tf_op jit(solution)/shard_map/convert_element_type | solution.py:583
  54.4 0.6 %copy.10 = f32[64,256]{1,0:T(8,128)} copy(f32[64,256]{1,0:T(8,128)S(1)} %get-tuple-element.26) | data formatting | bytes 131072
Async XLA Ops:
  0.6 0.8 %copy-start = (f32[64,256]{1,0:T(8,128)S(1)}, f32[64,256]{1,0:T(8,128)}, u32[]{:S(2)}) copy-start(f32[64,256]{1,0:T(8,128)} %taps_ref.1) | copy-start | bytes 196612

commit v7 on v6

--- a/solution.py
+++ b/solution.py
@@ -227,7 +227,6 @@
 
 TAPS_BLOCK = 128
 CHUNK_CH = 128
-LOAD_PIECES = 4
 MESH = pl.DeviceIdType.MESH
 NT = (((1,), (1,)), ((), ()))
 
@@ -253,18 +252,18 @@
     per_block = block // tokens
     chunk_groups = CHUNK_CH // GROUP_CH
 
-    offsets = []
-    for order in range(nch // 2):
-        far = nch // 2 + (-(order + 1) // 2 if order % 2 else order // 2)
-        offsets.append((far, (far + nch // 2) % nch))
-    partners = []
-    for pair in offsets:
+    rounds = []
+    for order in range(nch):
+        step = -(order + 1) // 2 if order % 2 else order // 2
+        offset = (nch // 2 + step) % nch
+        other_ch = lax.rem(ch + offset, nch)
+        turns = []
         for turn in range(1, nctx + 1):
-            for offset in pair:
-                if offset or turn < nctx:
-                    other_ch = lax.rem(ch + offset, nch)
-                    other_ctx = lax.rem(ctx + turn, nctx)
-                    partners.append((other_ctx, other_ch, other_ctx * nch + other_ch))
+            if offset or turn < nctx:
+                other_ctx = lax.rem(ctx + turn, nctx)
+                turns.append((other_ctx, other_ch, other_ctx * nch + other_ch))
+        rounds.append((other_ch, turns))
+    partners = [partner for _, turns in rounds for partner in turns]
 
     def columns(owner_ctx, owner_ch, chunk):
         start = owner_ch * (nctx * chans) + owner_ctx * chans + chunk * CHUNK_CH
@@ -278,8 +277,8 @@
             grad_ref[:, cols].astype(jnp.float32) * query_ref[:, cols].astype(jnp.float32)
         ).astype(jnp.bfloat16)
 
-    def send_in(chunk):
-        for other_ctx, other_ch, other in partners:
+    def send_in(chunk, turns):
+        for other_ctx, other_ch, other in turns:
             pltpu.make_async_remote_copy(
                 src_ref=staged.at[:, columns(other_ctx, other_ch, chunk)],
                 dst_ref=landed.at[chunk, me],
@@ -350,55 +349,41 @@
 
         lax.fori_loop(0, count, step, 0, unroll=unroll)
 
-    pieces = LOAD_PIECES
-    piece = nctx * nch * chans // pieces
-
-    def load(which, part):
+    def load(which, order):
         src, dst = (
-            (query_hbm, query_ref),
             (key_hbm, key_ref),
             (value_hbm, value_ref),
             (grad_hbm, grad_ref),
+            (query_hbm, query_ref),
         )[which]
-        cols = pl.ds(part * piece, piece)
-        return pltpu.make_async_copy(src.at[:, cols], dst.at[:, cols], load_sem.at[which, part])
-
-    for part in range(pieces):
-        for which in range(4):
-            load(which, part).start()
+        piece = nctx * chans
+        cols = pl.ds(pl.multiple_of(rounds[order][0] * piece, 128), piece)
+        return pltpu.make_async_copy(src.at[:, cols], dst.at[:, cols], load_sem.at[which, order])
 
     barrier = pltpu.get_barrier_semaphore()
-
     for other_ctx, other_ch, _ in partners:
         pl.semaphore_signal(barrier, inc=1, device_id=(other_ctx, other_ch), device_id_type=MESH)
-
-    def gate_chunk(chunk, first, count):
-        each(
-            count,
-            lambda n: gate(
-                pl.ds(pl.multiple_of((first + n) * chans + chunk * CHUNK_CH, 128), CHUNK_CH)
-            ),
-            unroll=4,
-        )
-
+    for order in range(nch):
+        for which in range(4):
+            load(which, order).start()
     own_taps = pltpu.make_async_copy(
         taps_ref.at[pl.ds(pl.multiple_of(ctx * groups, 8), groups), :],
         taps.at[:, pl.ds(pl.multiple_of(ctx * span, 128), span)],
         local_sem.at[3 * chunks],
     )
     own_taps.start()
-    for part in range(pieces):
-        for which in range(4):
-            load(which, part).wait()
-        gate_chunk(0, part * (ndev // pieces), ndev // pieces)
-    pl.semaphore_wait(barrier, ndev - 1)
-    for step in range(1, nctx):
-        tap_copy(step, True).start()
-    send_in(0)
-    own_in(0).start()
-    for chunk in range(1, chunks):
-        gate_chunk(chunk, 0, ndev)
-        send_in(chunk)
+    for chunk in range(chunks):
+        for order, (other_ch, turns) in enumerate(rounds):
+            if chunk == 0:
+                for which in range(4):
+                    load(which, order).wait()
+            for owner in range(nctx):
+                gate(columns(owner, other_ch, chunk))
+            if chunk == 0 and order == 0:
+                pl.semaphore_wait(barrier, ndev - 1)
+                for step in range(1, nctx):
+                    tap_copy(step, True).start()
+            send_in(chunk, turns)
         own_in(chunk).start()
     own_taps.wait()
     for step in range(1, nctx):
@@ -568,7 +553,7 @@
             sem((nctx,)),
             sem((nctx,)),
             sem((3 * chunks + 2,)),
-            sem((4, LOAD_PIECES)),
+            sem((4, nch)),
         ],
         compiler_params=pltpu.CompilerParams(
             collective_id=0, has_side_effects=True, vmem_limit_bytes=51 * 1024 * 1024

time: 55.4 us -> 55.7 us (level)
  no operation moved by 1% of the time
where the time goes in v7:
time: 55.7 us; the launch traced here: 55.5 us
  Pallas kernels  52.1 us (94%)
  local copies, waits for them, and re-layouts  1.46 us (3%)
  other arithmetic  1.35 us (2%)
  between operations  0.65 us (1%)
    pallas_call x1, Pallas kernels, one_exchange(): pl.pallas_call(functools.partial(exchange_kernel, nctx, nch, chunks), out...  52.1 us
    unnamed x3, local copies, waits for them, and re-layouts  1.46 us
    convert_element_type x1, other arithmetic, one_exchange(): (correlated * key_near.astype(jnp.float32)).astype(half)  1.35 us

profile of v7, /device:TPU:0, one launch (start us, length us, event | category | flops | bytes accessed | tf_op | source)
XLA Modules:
  0.0 55.5 jit_solution(221518240248429761)
XLA Ops:
  0.6 0.0 copy-start
  0.6 0.8 %copy-done = f32[64,256]{1,0:T(8,128)S(1)} copy-done((f32[64,256]{1,0:T(8,128)S(1)}, f32[64,256]{1,0:T(8,128)}, u32[]{:S(2)}) %copy-start) | copy-done | bytes 65560
  1.5 52.1 %exchange_and_convolve.1 = (bf16[32,8192]{1,0:T(8,128)(2,1)S(1)}, bf16[32,8192]{1,0:T(8,128)(2,1)S(1)}, f32[64,256]{1,0:T(8,128)S(1)}, bf16[32,8192]{1,0:T(8,128...) custom-call(bf16[32,8192]{1,0:T(8,128)(2,1)} %query_hbm.1, bf16[32,8192]{1,0:T(8,128)(2,1)} %key_hbm.1, ...), custom_call_target="tpu_custom_call" | custom-call | tf_op jit(solution)/shard_map/exchange_and_convolve/pallas_call | solution.py:525
  53.5 1.4 %fusion.1 = (bf16[32,8192]{1,0:T(8,128)(2,1)}, bf16[32,8192]{1,0:T(8,128)(2,1)}, bf16[32,8192]{1,0:T(8,128)(2,1)}) fusion(bf16[32,8192]{1,0:T(8,128)(2,1)S(1)} %get-tuple-element.12, bf16[32,8192]{1,0:T(8,128)(2,1)S(1)} %get-tuple-element.14, bf16[32,8192]{1,0:T(8,128)(2,1)S(1)} %get-tuple-element.13, bf16[32,8192]{1,0:T(8,128)(2,1)S(1)} %get-tuple-element.11, ...), kind=kLoop, calls=%fused_computation.3 | loop fusion | flops 2883584 | bytes 4194304 | tf_op jit(solution)/shard_map/convert_element_type | solution.py:568
  54.9 0.6 %copy.10 = f32[64,256]{1,0:T(8,128)} copy(f32[64,256]{1,0:T(8,128)S(1)} %get-tuple-element.26) | data formatting | bytes 131072
Async XLA Ops:
  0.6 0.8 %copy-start = (f32[64,256]{1,0:T(8,128)S(1)}, f32[64,256]{1,0:T(8,128)}, u32[]{:S(2)}) copy-start(f32[64,256]{1,0:T(8,128)} %taps_ref.1) | copy-start | bytes 196612

commit v8 on v6

--- a/solution.py
+++ b/solution.py
@@ -575,14 +575,28 @@
         ),
         name="exchange_and_convolve",
     )(query_gate, key_gate, value_proj, grad_out, long_filters)
-    convolved = convolved.astype(jnp.float32)
-    correlated = correlated.astype(jnp.float32)
-    return (
-        (grad_near.astype(jnp.float32) * convolved).astype(half),
-        (correlated * value_near.astype(jnp.float32)).astype(half),
-        (correlated * key_near.astype(jnp.float32)).astype(half),
-        grad_filters,
-    )
+    steps = 4
+    part = pl.BlockSpec((tokens, model // steps), lambda i: (0, i))
+    share = pl.BlockSpec((long_filters.shape[0] // steps, long_filters.shape[1]), lambda i: (i, 0))
+    return pl.pallas_call(
+        finish_kernel,
+        grid=(steps,),
+        out_shape=(jax.ShapeDtypeStruct((tokens, model), half),) * 3
+        + (jax.ShapeDtypeStruct(long_filters.shape, jnp.float32),),
+        in_specs=[part] * 5 + [share],
+        out_specs=(part, part, part, share),
+        name="multiply_gates",
+    )(convolved, correlated, key_near, value_near, grad_near, grad_filters)
+
+
+def finish_kernel(conv, corr, key, value, grad, filt, grad_query, grad_key, grad_value, grad_filt):
+    back = corr[...].astype(jnp.float32)
+    grad_query[...] = (grad[...].astype(jnp.float32) * conv[...].astype(jnp.float32)).astype(
+        jnp.bfloat16
+    )
+    grad_key[...] = (back * value[...].astype(jnp.float32)).astype(jnp.bfloat16)
+    grad_value[...] = (back * key[...].astype(jnp.float32)).astype(jnp.bfloat16)
+    grad_filt[...] = filt[...]
 
 
 def fits_one_exchange(nctx, nch, query_shape, filter_shape):

time: 55.4 us -> 61.9 us (1.12)
  local copies, waits for them, and re-layouts: 1.46 us -> 5.42 us
  Pallas kernels: 51.6 us -> 55.4 us
  other arithmetic: 1.35 us -> 0 us
    unnamed x3 -> x14, local copies, waits for them, and re-layouts: 1.46 us -> 5.42 us
    pallas_call x0 -> x1, Pallas kernels: none -> 3.85 us  [one_exchange(): pl.pallas_call(finish_kernel, grid=(steps,), out_shape=(jax.ShapeDtypeStr...]
    convert_element_type x1 -> x0, other arithmetic: 1.35 us -> none  [one_exchange(): (correlated * key_near.astype(jnp.float32)).astype(half)]
where the time goes in v8:
time: 61.9 us; the launch traced here: 61.5 us
  Pallas kernels  55.4 us (89%)
  local copies, waits for them, and re-layouts  5.42 us (9%)
  between operations  0.66 us (1%)
    pallas_call x1, Pallas kernels, one_exchange(): pl.pallas_call(functools.partial(exchange_kernel, nctx, nch, chunks), out...  51.6 us
    unnamed x14, local copies, waits for them, and re-layouts  5.42 us
    pallas_call x1, Pallas kernels, one_exchange(): pl.pallas_call(finish_kernel, grid=(steps,), out_shape=(jax.ShapeDtypeStr...  3.85 us

profile of v8, /device:TPU:0, one launch (start us, length us, event | category | flops | bytes accessed | tf_op | source)
XLA Modules:
  0.0 61.5 jit_solution(18373620227153859508)
XLA Ops:
  0.6 0.0 copy-start.5
  0.6 0.8 %copy-done.5 = f32[64,256]{1,0:T(8,128)S(1)} copy-done((f32[64,256]{1,0:T(8,128)S(1)}, f32[64,256]{1,0:T(8,128)}, u32[]{:S(2)}) %copy-start.5) | copy-done | bytes 65560
  1.5 51.6 %exchange_and_convolve.1 = (bf16[32,8192]{1,0:T(8,128)(2,1)S(1)}, bf16[32,8192]{1,0:T(8,128)(2,1)S(1)}, f32[64,256]{1,0:T(8,128)S(1)}, bf16[32,8192]{1,0:T(8,128...) custom-call(bf16[32,8192]{1,0:T(8,128)(2,1)} %query_hbm.1, bf16[32,8192]{1,0:T(8,128)(2,1)} %key_hbm.1, ...), custom_call_target="tpu_custom_call" | custom-call | tf_op jit(solution)/shard_map/exchange_and_convolve/pallas_call | solution.py:540
  53.1 0.0 copy-start
  53.1 0.8 %copy-done = bf16[32,8192]{1,0:T(8,128)(2,1)} copy-done((bf16[32,8192]{1,0:T(8,128)(2,1)}, bf16[32,8192]{1,0:T(8,128)(2,1)S(1)}, u32[]{:S(2)}) %copy-start) | copy-done | bytes 524312
  53.9 0.0 copy-start.1
  53.9 0.8 %copy-done.1 = bf16[32,8192]{1,0:T(8,128)(2,1)} copy-done((bf16[32,8192]{1,0:T(8,128)(2,1)}, bf16[32,8192]{1,0:T(8,128)(2,1)S(1)}, u32[]{:S(2)}) %copy-start.1) | copy-done | bytes 524312
  54.6 0.0 copy-start.2
  54.6 0.8 %copy-done.2 = bf16[32,8192]{1,0:T(8,128)(2,1)} copy-done((bf16[32,8192]{1,0:T(8,128)(2,1)}, bf16[32,8192]{1,0:T(8,128)(2,1)S(1)}, u32[]{:S(2)}) %copy-start.2) | copy-done | bytes 524312
  55.5 0.0 copy-start.3
  55.5 0.8 %copy-done.3 = bf16[32,8192]{1,0:T(8,128)(2,1)} copy-done((bf16[32,8192]{1,0:T(8,128)(2,1)}, bf16[32,8192]{1,0:T(8,128)(2,1)S(1)}, u32[]{:S(2)}) %copy-start.3) | copy-done | bytes 524312
  56.3 0.0 copy-start.4
  56.3 0.8 %copy-done.4 = bf16[32,8192]{1,0:T(8,128)(2,1)} copy-done((bf16[32,8192]{1,0:T(8,128)(2,1)}, bf16[32,8192]{1,0:T(8,128)(2,1)S(1)}, u32[]{:S(2)}) %copy-start.4) | copy-done | bytes 524312
  57.1 0.0 copy-start.6
  57.1 0.6 copy-done.6
  57.7 3.8 %multiply_gates.1 = (bf16[32,8192]{1,0:T(8,128)(2,1)}, bf16[32,8192]{1,0:T(8,128)(2,1)}, bf16[32,8192]{1,0:T(8,128)(2,1)}, f32[64,256]{1,0:T(8,128)}) custom-call(bf16[32,8192]{1,0:T(8,128)(2,1)} %copy-done, bf16[32,8192]{1,0:T(8,128)(2,1)} %copy-done.1, bf16[32,8192]{1,0:T(8,128)(2,1)} %copy-done.2, bf16[32,8192]{1,0:T(8,128)(2,1)} %copy-done.3, ...), custom_call_target="tpu_custom_call" | custom-call | tf_op jit(solution)/shard_map/multiply_gates/pallas_call | solution.py:581
Async XLA Ops:
  0.6 0.8 %copy-start.5 = (f32[64,256]{1,0:T(8,128)S(1)}, f32[64,256]{1,0:T(8,128)}, u32[]{:S(2)}) copy-start(f32[64,256]{1,0:T(8,128)} %taps_ref.1) | copy-start | bytes 196612
  53.1 0.8 %copy-start = (bf16[32,8192]{1,0:T(8,128)(2,1)}, bf16[32,8192]{1,0:T(8,128)(2,1)S(1)}, u32[]{:S(2)}) copy-start(bf16[32,8192]{1,0:T(8,128)(2,1)S(1)} %get-tuple-element.10.conv) | copy-start | bytes 1572868
  53.9 0.8 %copy-start.1 = (bf16[32,8192]{1,0:T(8,128)(2,1)}, bf16[32,8192]{1,0:T(8,128)(2,1)S(1)}, u32[]{:S(2)}) copy-start(bf16[32,8192]{1,0:T(8,128)(2,1)S(1)} %get-tuple-element.11.corr) | copy-start | bytes 1572868
  54.6 0.8 %copy-start.2 = (bf16[32,8192]{1,0:T(8,128)(2,1)}, bf16[32,8192]{1,0:T(8,128)(2,1)S(1)}, u32[]{:S(2)}) copy-start(bf16[32,8192]{1,0:T(8,128)(2,1)S(1)} %get-tuple-element.12.key) | copy-start | bytes 1572868
  55.5 0.8 %copy-start.3 = (bf16[32,8192]{1,0:T(8,128)(2,1)}, bf16[32,8192]{1,0:T(8,128)(2,1)S(1)}, u32[]{:S(2)}) copy-start(bf16[32,8192]{1,0:T(8,128)(2,1)S(1)} %get-tuple-element.13.value) | copy-start | bytes 1572868
  56.3 0.8 %copy-start.4 = (bf16[32,8192]{1,0:T(8,128)(2,1)}, bf16[32,8192]{1,0:T(8,128)(2,1)S(1)}, u32[]{:S(2)}) copy-start(bf16[32,8192]{1,0:T(8,128)(2,1)S(1)} %get-tuple-element.14.grad) | copy-start | bytes 1572868
  57.1 0.6 copy-start.6
